TPU v7x, 256 devices: a whole 4x4x8 slice. The times are simulated.
256 devices in a mesh: tok: 64 (over y, z, core), head: 4 (over x).
Axes of the slice: x: 4, y: 4, z: 8, core: 2. Of those that a mesh axis runs over, the one named last changes fastest.
Arguments:
- tokens: bfloat16 [16384, 1024], P('tok'), may hold values from -6 to 6
- gain_one: float32 [1024], replicated, may hold values from 0.5 to 1.5
- qkv_one: bfloat16 [3, 1024, 1024], P(None, None, 'head'), may hold values from -0.1875 to 0.1875
- out_one: bfloat16 [1024, 1024], P('head'), may hold values from -0.1875 to 0.1875
- gain_two: float32 [1024], replicated, may hold values from 0.5 to 1.5
- qkv_two: bfloat16 [3, 1024, 1024], P(None, None, 'head'), may hold values from -0.1875 to 0.1875
- out_two: bfloat16 [1024, 1024], P('head'), may hold values from -0.1875 to 0.1875
- hilbert_pos: int32 [16384], replicated, may hold values from 0 to 16383, as said below
- scene: int32 [16384], replicated, may hold values from 0 to 127, never falling along the last dimension, each value on 1 to 256 neighbouring positions
- cotangent: bfloat16 [16384, 1024], P('tok'), may hold values from -16 to 16
Outputs:
- grad_input: bfloat16 [16384, 1024], P('tok')
- qkv_grad_one: float32 [3, 1024, 1024], P(None, 'tok', 'head')
- out_grad_one: float32 [1024, 1024], P('tok', 'head')
- gain_grad_one: float32 [1024], P('tok')
- qkv_grad_two: float32 [3, 1024, 1024], P(None, 'tok', 'head')
- out_grad_two: float32 [1024, 1024], P('tok', 'head')
- gain_grad_two: float32 [1024], P('tok')
Inputs may be any that keep to these rules, and one draw needn't show every extreme that they name: `hilbert_pos`: A permutation. Of the 256 Z positions k * 256 to (k + 1) * 256 - 1, at most 8 have Hilbert positions in one block m * 256 to (m + 1) * 256 - 1, and in every draw some pair of blocks reaches 8.
All inputs are finite; a program needn't handle non-finite values.
Results may differ from a plain program's by a relative error of at most 0.023.
Values may be sent and summed in bfloat16 or wider, within the bound.
A program may use at most 64 MiB of HBM per device.

v0:
```python
import math

import jax
import jax.numpy as jnp
from jax import lax
from jax.sharding import PartitionSpec as P

HEAD_DIM = 64


NORM_EPS = 1e-06


def partner(value, axis, apart):
    mask = 2**apart
    pairs = [(source, source ^ mask) for source in range(lax.axis_size(axis))]
    return lax.ppermute(value, axis, pairs)


def normalize(layer_in, gain_vec):
    wide_in = layer_in.astype(jnp.float32)
    inv_rms = lax.rsqrt(jnp.mean(wide_in * wide_in, axis=-1, keepdims=True) + NORM_EPS)
    return ((wide_in * inv_rms * gain_vec).astype(jnp.bfloat16), inv_rms)


def project(normed, matrix):
    return jnp.dot(normed, matrix, preferred_element_type=jnp.float32).astype(jnp.bfloat16)


def mix_heads(partial_sum):
    return lax.psum(partial_sum, "head")


def relayout(outgoing):
    return lax.all_to_all(outgoing, "tok", split_axis=0, concat_axis=0, tiled=True)


def window_join(own_rows, other_rows, parity):
    return jnp.where(
        parity == 0,
        jnp.concatenate([own_rows, other_rows], 0),
        jnp.concatenate([other_rows, own_rows], 0),
    )


def layer_front(layer_in, gain_vec, qkv_mat, allowed, parity):
    tok_rows = layer_in.shape[0]
    head_count = qkv_mat.shape[2] // HEAD_DIM
    normed, inv_rms = normalize(layer_in, gain_vec)
    queries = project(normed, qkv_mat[0])
    keys_own = project(normed, qkv_mat[1])
    values_own = project(normed, qkv_mat[2])
    keys_other, values_other = partner((keys_own, values_own), "tok", 0)
    keys_win = window_join(keys_own, keys_other, parity).reshape(2 * tok_rows, head_count, HEAD_DIM)
    values_win = window_join(values_own, values_other, parity).reshape(
        2 * tok_rows, head_count, HEAD_DIM
    )
    q_heads = queries.reshape(tok_rows, head_count, HEAD_DIM)
    scores = jnp.einsum("qhd,khd->hqk", q_heads, keys_win, preferred_element_type=jnp.float32)
    scores = scores * (1.0 / math.sqrt(HEAD_DIM))
    weights_exp = jnp.exp(scores)
    if allowed is not None:
        weights_exp = jnp.where(allowed[None], weights_exp, 0.0)
    probs_full = weights_exp / jnp.sum(weights_exp, axis=-1, keepdims=True)
    probs_low = probs_full.astype(jnp.bfloat16)
    mixed = jnp.einsum("hqk,khd->qhd", probs_low, values_win, preferred_element_type=jnp.float32)
    attn_out = mixed.astype(jnp.bfloat16).reshape(tok_rows, head_count * HEAD_DIM)
    return (normed, inv_rms, q_heads, keys_win, values_win, probs_full, probs_low, attn_out)


def layer_back(layer_in, gain_vec, qkv_mat, out_mat, cot_in, saved, parity, grad_scale):
    normed, inv_rms, q_heads, keys_win, values_win, probs_full, probs_low, attn_out = saved
    tok_rows = layer_in.shape[0]
    head_cols = qkv_mat.shape[2]
    out_grad = (
        jnp.einsum("te,tc->ec", cot_in, attn_out, preferred_element_type=jnp.float32) * grad_scale
    )
    d_out = jnp.einsum("te,ce->tc", cot_in, out_mat, preferred_element_type=jnp.float32).astype(
        jnp.bfloat16
    )
    d_heads = d_out.reshape(q_heads.shape)
    d_probs = jnp.einsum("qhd,khd->hqk", d_heads, values_win, preferred_element_type=jnp.float32)
    d_values_win = jnp.einsum(
        "hqk,qhd->khd", probs_low, d_heads, preferred_element_type=jnp.float32
    )
    d_scores = probs_full * (d_probs - jnp.sum(d_probs * probs_full, axis=-1, keepdims=True))
    d_low = (d_scores * (1.0 / math.sqrt(HEAD_DIM))).astype(jnp.bfloat16)
    d_queries = jnp.einsum("hqk,khd->qhd", d_low, keys_win, preferred_element_type=jnp.float32)
    d_queries = d_queries.astype(jnp.bfloat16).reshape(tok_rows, head_cols)
    d_keys_win = jnp.einsum("hqk,qhd->khd", d_low, q_heads, preferred_element_type=jnp.float32)
    first_half = parity == 0
    keys_mine = jnp.where(first_half, d_keys_win[:tok_rows], d_keys_win[tok_rows:])
    keys_theirs = jnp.where(first_half, d_keys_win[tok_rows:], d_keys_win[:tok_rows])
    values_mine = jnp.where(first_half, d_values_win[:tok_rows], d_values_win[tok_rows:])
    values_theirs = jnp.where(first_half, d_values_win[tok_rows:], d_values_win[:tok_rows])
    keys_back, values_back = (
        partner(keys_theirs.astype(jnp.bfloat16), "tok", 0).astype(keys_theirs.dtype),
        partner(values_theirs.astype(jnp.bfloat16), "tok", 0).astype(values_theirs.dtype),
    )
    d_keys = (keys_mine + keys_back).astype(jnp.bfloat16).reshape(tok_rows, head_cols)
    d_values = (values_mine + values_back).astype(jnp.bfloat16).reshape(tok_rows, head_cols)
    qkv_grad = (
        jnp.stack(
            [
                jnp.einsum("td,tc->dc", normed, d_queries, preferred_element_type=jnp.float32),
                jnp.einsum("td,tc->dc", normed, d_keys, preferred_element_type=jnp.float32),
                jnp.einsum("td,tc->dc", normed, d_values, preferred_element_type=jnp.float32),
            ]
        )
        * grad_scale
    )
    d_part = jnp.einsum("tc,dc->td", d_queries, qkv_mat[0], preferred_element_type=jnp.float32)
    d_part = d_part + jnp.einsum(
        "tc,dc->td", d_keys, qkv_mat[1], preferred_element_type=jnp.float32
    )
    d_part = d_part + jnp.einsum(
        "tc,dc->td", d_values, qkv_mat[2], preferred_element_type=jnp.float32
    )
    wide_in = layer_in.astype(jnp.float32)
    d_normed = mix_heads(d_part)
    gain_grad = jnp.sum(d_normed * wide_in * inv_rms, axis=0) * grad_scale
    d_scaled = d_normed * gain_vec
    d_input = cot_in.astype(jnp.float32) + inv_rms * (
        d_scaled
        - wide_in * inv_rms * inv_rms * jnp.mean(d_scaled * wide_in, axis=-1, keepdims=True)
    )
    grad_sums = (
        lax.psum_scatter(qkv_grad, "tok", scatter_dimension=1, tiled=True),
        lax.psum_scatter(out_grad, "tok", scatter_dimension=0, tiled=True),
        lax.psum_scatter(gain_grad, "tok", scatter_dimension=0, tiled=True),
    )
    return (d_input.astype(jnp.bfloat16), grad_sums)


def local(
    tokens, gain_one, qkv_one, out_one, gain_two, qkv_two, out_two, hilbert_pos, scene, cotangent
):
    tok_rows = tokens.shape[0]
    feat_width = tokens.shape[1]
    tok_count = lax.axis_size("tok")
    tok_index = lax.axis_index("tok")
    parity = tok_index % 2
    grad_scale = 1.0 / math.sqrt(tok_rows * tok_count)
    slot_cap = 2 * tok_rows // tok_count
    total = hilbert_pos.shape[0]
    own_hilbert = lax.dynamic_slice_in_dim(hilbert_pos, tok_index * tok_rows, tok_rows)
    target = own_hilbert // tok_rows
    onehot = (target[:, None] == jnp.arange(tok_count, dtype=jnp.int32)[None, :]).astype(jnp.int32)
    send_slot = jnp.sum((jnp.cumsum(onehot, axis=0) - onehot) * onehot, axis=1)
    inverse = jnp.zeros_like(hilbert_pos).at[hilbert_pos].set(jnp.arange(total, dtype=jnp.int32))
    own_zpos = lax.dynamic_slice_in_dim(inverse, tok_index * tok_rows, tok_rows)
    source = own_zpos // tok_rows
    earlier = (source[:, None] == source[None, :]) & (own_zpos[None, :] < own_zpos[:, None])
    recv_slot = jnp.sum(earlier.astype(jnp.int32), axis=1)
    saved_one = layer_front(tokens, gain_one, qkv_one, None, parity)
    attn_mix = jnp.dot(saved_one[7], out_one, preferred_element_type=jnp.float32)
    full_mix = mix_heads(attn_mix)
    first_out = (tokens.astype(jnp.float32) + full_mix).astype(jnp.bfloat16)
    outgoing = (
        jnp.zeros((tok_count, slot_cap, feat_width), jnp.bfloat16)
        .at[target, send_slot]
        .set(first_out)
    )
    second_in = relayout(outgoing)[source, recv_slot]
    window_start = tok_index // 2 * (2 * tok_rows)
    scene_win = lax.dynamic_slice_in_dim(scene, window_start, 2 * tok_rows)
    scene_own = lax.dynamic_slice_in_dim(scene, tok_index * tok_rows, tok_rows)
    allowed = scene_own[:, None] == scene_win[None, :]
    saved_two = layer_front(second_in, gain_two, qkv_two, allowed, parity)
    d_second, sums_two = layer_back(
        second_in, gain_two, qkv_two, out_two, cotangent, saved_two, parity, grad_scale
    )
    back_width = d_second.shape[1]
    returned = (
        jnp.zeros((tok_count, slot_cap, back_width), jnp.bfloat16)
        .at[source, recv_slot]
        .set(d_second)
    )
    d_first = relayout(returned)[target, send_slot]
    grad_input, sums_one = layer_back(
        tokens, gain_one, qkv_one, out_one, d_first, saved_one, parity, grad_scale
    )
    return (
        grad_input,
        sums_one[0],
        sums_one[1],
        sums_one[2],
        sums_two[0],
        sums_two[1],
        sums_two[2],
    )


def solution(mesh):
    in_specs = (
        P("tok", None),
        P(),
        P(None, None, "head"),
        P("head", None),
        P(),
        P(None, None, "head"),
        P("head", None),
        P(),
        P(),
        P("tok", None),
    )
    out_specs = (
        P("tok", None),
        P(None, "tok", "head"),
        P("tok", "head"),
        P("tok"),
        P(None, "tok", "head"),
        P("tok", "head"),
        P("tok"),
    )
    return jax.shard_map(local, mesh=mesh, in_specs=in_specs, out_specs=out_specs, check_vma=False)
```

profile of v0, /device:TPU:8, one launch (start us, length us, event | category | flops | bytes accessed | tf_op | source)
XLA Modules:
  0.0 968.5 jit_solution(3894416438079937393)
XLA Ops:
  8.6 1.7 convolution_convert_fusion.5
  16.0 60.3 %scatter_custom_fusion = s32[16384]{0:T(1024)S(1)} fusion(s32[16384]{0:T(1024)S(1)} %compare_select_fusion, s32[16384]{0:T(1024)S(1)} %iota.11, s32[]{:T(128)} %constant.67.clone.1), kind=kCustom, calls=%fused_computation.150 | custom fusion | bytes 65540 | tf_op jit(solution)/shard_map/scatter | solution.py:150
  79.9 36.2 %scatter_fusion = bf16[64,8,1024]{2,1,0:T(8,128)(2,1)} fusion(bf16[64,8,1024]{2,1,0:T(8,128)(2,1)} %broadcast.159.clone, s32[256]{0:T(256)S(1)} %bitcast.141, bf16[256,1024]{1,0:T(8,128)(2,1)S(1)} %fusion.58), kind=kCustom, calls=%fused_computation.3 | custom fusion | bytes 1574912 | tf_op jit(solution)/shard_map/scatter | solution.py:162
  116.1 12.2 %all-to-all-start = ((bf16[64,8,1024]{2,1,0:T(8,128)(2,1)}), bf16[64,8,1024]{2,1,0:T(8,128)(2,1)S(1)}, u32[]{:S(2)}, u32[]{:S(2)}) async-start(bf16[64,8,1024]{2,1,0:T(8,128)(2,1)} %scatter_fusion), calls=%async_computation | async-start | bytes 2097152 | tf_op jit(solution)/shard_map/all_to_all | solution.py:35
  130.7 24.8 %all-to-all-done = bf16[64,8,1024]{2,1,0:T(8,128)(2,1)S(1)} async-done(((bf16[64,8,1024]{2,1,0:T(8,128)(2,1)}), bf16[64,8,1024]{2,1,0:T(8,128)(2,1)S(1)}, u32[]{:S(2)}, u32[]{:S(2)}) %all-to-all-start) | async-done | bytes 1048608 | tf_op jit(solution)/shard_map/all_to_all | solution.py:35
  155.4 2.7 gather_fusion
  158.4 1.6 convolution_convert_fusion.4
  160.4 1.5 collective-permute-start.2
  165.0 1.8 fusion.100
  166.9 9.1 fusion.32
  176.0 9.0 fusion.38
  185.8 1.4 fusion.68
  189.7 48.3 %all-reduce.9.cloned.1.call-done = f32[256,1024]{1,0:T(8,128)} async-done(((f32[256,1024]{1,0:T(8,128)}), f32[256,1024]{1,0:T(8,128)}) %all-reduce.9.cloned.1.call-update) | async-done | bytes 1048592 | tf_op jit(solution)/shard_map/psum | solution.py:31
  238.1 2.2 fusion.56
  241.6 25.3 %scatter_fusion.1 = bf16[64,8,1024]{2,1,0:T(8,128)(2,1)S(1)} fusion(bf16[64,8,1024]{2,1,0:T(8,128)(2,1)S(1)} %broadcast.159, s32[256]{0:T(256)S(1)} %bitcast.140, bf16[256,1024]{1,0:T(8,128)(2,1)} %fusion.52), kind=kCustom, calls=%fused_computation.4 | custom fusion | bytes 1574912 | tf_op jit(solution)/shard_map/scatter | solution.py:177
  266.9 37.5 %all_to_all.10 = bf16[64,8,1024]{2,1,0:T(8,128)(2,1)S(1)} all-to-all(bf16[64,8,1024]{2,1,0:T(8,128)(2,1)S(1)} %scatter_fusion.1), channel_id=1, replica_groups=mesh['tok'=64,'head'=4] {'tok'}, dimensions={0} | all-to-all | bytes 2097152 | tf_op jit(solution)/shard_map/all_to_all | solution.py:35
  304.4 2.7 gather_fusion.1
  307.5 2.2 convolution_bitcast_fusion.6
  309.7 1.8 fusion.103
  311.5 8.4 fusion.29
  319.9 8.9 fusion.35
  328.9 1.5 collective-permute-start.7
  334.5 2.6 convolution_convert_fusion.8
  341.7 1.9 maximum_multiply_fusion.1
  346.0 2.0 maximum_multiply_fusion
  349.9 32.6 %all-reduce.11.cloned.1.call-done = f32[256,1024]{1,0:T(8,128)} async-done(((f32[256,1024]{1,0:T(8,128)}), f32[256,1024]{1,0:T(8,128)}) %all-reduce.11.cloned.1.call-update) | async-done | bytes 1048592 | tf_op jit(solution)/shard_map/psum | solution.py:31
  382.5 1.6 fusion.61
  384.2 108.1 %all-reduce.2 = (f32[1024]{0:T(1024)S(1)}, f32[1024]{0:T(1024)S(1)}) all-reduce(f32[1024]{0:T(1024)S(1)} %broadcast_multiply_fusion.1, f32[1024]{0:T(1024)S(1)} %broadcast_multiply_fusion), channel_id=4, replica_groups=mesh['tok'=64,'head'=4] {'tok'}, use_global_device_ids=true, to_apply=%region_21.22.clone | all-reduce | flops 2048 | bytes 16384
  494.7 32.4 %reduce-scatter.13.cloned.1.call-done = f32[16,256]{1,0:T(8,128)} async-done(((f32[1024,256]{1,0:T(8,128)}), f32[16,256]{1,0:T(8,128)}) %reduce-scatter.13.cloned.1.call-update) | async-done | bytes 16400
  527.0 142.7 %reduce-scatter.9.cloned.1.call-done = f32[16,256]{1,0:T(8,128)} async-done(((f32[1024,256]{1,0:T(8,128)}), f32[16,256]{1,0:T(8,128)}) %reduce-scatter.9.cloned.1.call-update) | async-done | bytes 16400 | tf_op jit(solution)/shard_map/reduce_scatter | solution.py:129
  669.7 145.7 %reduce-scatter.11.cloned.1.call-done = f32[3,16,256]{2,1,0:T(8,128)} async-done(((f32[3,1024,256]{2,1,0:T(8,128)}), f32[3,16,256]{2,1,0:T(8,128)}) %reduce-scatter.11.cloned.1.call-update) | async-done | bytes 49168 | tf_op jit(solution)/shard_map/reduce_scatter | solution.py:128
  815.4 145.8 %reduce-scatter.7.cloned.1.call-done = f32[3,16,256]{2,1,0:T(8,128)} async-done(((f32[3,1024,256]{2,1,0:T(8,128)}), f32[3,16,256]{2,1,0:T(8,128)}) %reduce-scatter.7.cloned.1.call-update) | async-done | bytes 49168 | tf_op jit(solution)/shard_map/reduce_scatter | solution.py:128
  (191 shorter events, 35.9 us)
Async XLA Ops:
  7.2 7.4 copy-start
  7.2 3.3 copy-start.1
  7.2 3.2 copy-start.28
  7.2 3.2 copy-start.9
  7.2 70.2 %all-reduce.7.cloned.1.call-start = ((), (), s32[]{:S(2)}) async-start(), calls=%async_computation.6 | async-start | bytes 2097152 | tf_op jit(solution)/shard_map/psum | solution.py:31
  10.3 1.6 collective-permute-start.1
  10.9 1.7 collective-permute-start
  116.1 14.2 %copy-start.3 = (bf16[256,1024]{1,0:T(8,128)(2,1)S(1)}, bf16[256,1024]{1,0:T(8,128)(2,1)}, u32[]{:S(2)}) copy-start(bf16[256,1024]{1,0:T(8,128)(2,1)} %param.19) | copy-start | bytes 1572868
  116.1 14.2 %copy-start.15 = (bf16[256,1024]{1,0:T(8,128)(2,1)S(1)}, bf16[256,1024]{1,0:T(8,128)(2,1)}, u32[]{:S(2)}) copy-start(bf16[256,1024]{1,0:T(8,128)(2,1)} %param.16) | copy-start | bytes 1572868
  116.1 39.4 %all-to-all-start = ((bf16[64,8,1024]{2,1,0:T(8,128)(2,1)}), bf16[64,8,1024]{2,1,0:T(8,128)(2,1)S(1)}, u32[]{:S(2)}, u32[]{:S(2)}) async-start(bf16[64,8,1024]{2,1,0:T(8,128)(2,1)} %scatter_fusion), calls=%async_computation | async-start | bytes 2097152 | tf_op jit(solution)/shard_map/all_to_all | solution.py:35
  128.3 109.8 %all-reduce.9.cloned.1.call-start = ((), (), s32[]{:S(2)}) async-start(), calls=%async_computation.7 | async-start | bytes 2097152 | tf_op jit(solution)/shard_map/psum | solution.py:31
  130.3 45.7 %copy-start.22 = (pred[256,512]{1,0:T(8,128)(4,1)}, pred[256,512]{1,0:T(8,128)(4,1)S(1)}, u32[]{:S(2)}) copy-start(pred[256,512]{1,0:T(8,128)(4,1)S(1)} %broadcast_compare_fusion) | copy-start | bytes 393220
  158.3 81.9 %copy-start.30 = (f32[256]{0:T(256)}, f32[256]{0:T(256)S(1)}, u32[]{:S(2)}) copy-start(f32[256]{0:T(256)S(1)} %add_rsqrt_fusion) | copy-start | bytes 3076
  160.4 4.6 copy-start.25
  160.4 2.5 collective-permute-start.2
  161.9 3.1 collective-permute-start.3
  163.7 12.3 %copy-start.47 = (f32[4,256]{1,0:T(4,128)}, f32[4,256]{1,0:T(4,128)S(1)}, u32[]{:S(2)}) copy-start(f32[4,256]{1,0:T(4,128)S(1)} %get-tuple-element.52) | copy-start | bytes 12292
  165.0 20.0 %copy-start.11 = (f32[512,4,64]{0,2,1:T(8,128)}, f32[512,4,64]{0,2,1:T(8,128)S(1)}, u32[]{:S(2)}) copy-start(f32[512,4,64]{0,2,1:T(8,128)S(1)} %convolution_bitcast_fusion.7) | copy-start | bytes 1572868
  165.0 11.0 %copy-start.26 = (bf16[256,256]{0,1:T(8,128)(2,1)}, bf16[256,256]{0,1:T(8,128)(2,1)S(1)}, u32[]{:S(2)}) copy-start(bf16[256,256]{0,1:T(8,128)(2,1)S(1)} %collective-permute-done.3) | copy-start | bytes 393220
  166.9 9.2 copy-start.38
  185.1 2.6 collective-permute-start.5
  185.5 1.7 collective-permute-start.4
  189.7 192.9 %all-reduce.11.cloned.1.call-start = ((), (), s32[]{:S(2)}) async-start(), calls=%async_computation.8 | async-start | bytes 2097152 | tf_op jit(solution)/shard_map/psum | solution.py:31
  311.5 8.4 copy-start.34
  311.5 8.4 copy-start.36
  328.9 3.5 collective-permute-start.7
  330.4 1.5 collective-permute-start.6
  334.4 192.6 %reduce-scatter.13.cloned.1.call-start = ((), (), s32[]{:S(2)}) async-start(), calls=%async_computation.12 | async-start | bytes 1064960
  338.9 330.8 %reduce-scatter.9.cloned.1.call-start = ((), (), s32[]{:S(2)}) async-start(), calls=%async_computation.10 | async-start | bytes 1064960 | tf_op jit(solution)/shard_map/reduce_scatter | solution.py:129
  340.3 475.1 %reduce-scatter.11.cloned.1.call-start = ((), (), s32[]{:S(2)}) async-start(), calls=%async_computation.11 | async-start | bytes 3194880 | tf_op jit(solution)/shard_map/reduce_scatter | solution.py:128
  343.6 617.6 %reduce-scatter.7.cloned.1.call-start = ((), (), s32[]{:S(2)}) async-start(), calls=%async_computation.9 | async-start | bytes 3194880 | tf_op jit(solution)/shard_map/reduce_scatter | solution.py:128
  382.5 111.0 %copy-start.5 = (f32[256,1024]{1,0:T(8,128)S(1)}, f32[256,1024]{1,0:T(8,128)}, u32[]{:S(2)}) copy-start(f32[256,1024]{1,0:T(8,128)} %all-reduce.11.cloned.1.call-done) | copy-start | bytes 3145732
  (33 other events, 55.7 us)
Sparse Core Ops, SparseCore 0:
  16.0 53.7 all-reduce.6
  189.8 48.2 all-reduce.8
  334.6 47.9 all-reduce.10
  387.5 139.5 reduce-scatter.12
  532.0 137.6 reduce-scatter.8
  674.8 140.5 reduce-scatter.10
  820.6 140.5 reduce-scatter.6
where the time goes:
time: 981 us; the launch traced here: 968 us
  waiting for transfers between devices  573 us (58%)
  blocking collectives  146 us (15%)
  local copies, waits for them, and re-layouts  138 us (14%)
  matrix products  64 us (7%)
  starting transfers between devices  17.2 us (2%)
  between operations  16.1 us (2%)
  other arithmetic  14.6 us (1%)
    reduce_scatter x2, waiting for transfers between devices, layer_back(): lax.psum_scatter(qkv_grad, 'tok', scatter_dimension=1, tiled=True)  292 us
    reduce_scatter x1, waiting for transfers between devices, layer_back(): lax.psum_scatter(out_grad, 'tok', scatter_dimension=0, tiled=True)  143 us
    unnamed x1, blocking collectives  108 us
    psum x3, waiting for transfers between devices, mix_heads(): return lax.psum(partial_sum, 'head')  81 us
    scatter x1, local copies, waits for them, and re-layouts, local(): jnp.zeros_like(hilbert_pos).at[hilbert_pos]  60.3 us
    all_to_all x1, blocking collectives, relayout(): lax.all_to_all(outgoing, 'tok', split_axis=0, concat_axis=0, tiled=True)  37.5 us
    scatter x1, local copies, waits for them, and re-layouts, local(): outgoing = jnp.zeros((tok_count, slot_cap, feat_width), jnp.bfloat16).at[...  36.2 us
    unnamed x8, waiting for transfers between devices  32.5 us
  transfers between devices with their start and end apart: 16, of which 8 were waited for; matrix products, arithmetic and copies ran while one was open for 9% of the time, Pallas kernels for 0%

commit v1 on v0

v1 whole, which is shorter than its diff:
```python
import jax
import jax.numpy as jnp
from jax import lax
from jax.experimental import pallas as pl
from jax.experimental.pallas import tpu as pltpu
from jax.sharding import PartitionSpec as P

MESH = pl.DeviceIdType.MESH
F32 = jnp.float32
BF16 = jnp.bfloat16
EPS = 1e-06
ROWS = 256
BLK = 256
NX = 4
NT = 64
NY = 4
NZ = 8
HEADS = 4
HD = 64
SLOTS = 8
GRAD_SCALE = 1.0 / 128.0

KV = 0
BACK = 2
RS = 4
ROWSUM = 16
AG = 24
A2A = 36
GC = 38
GY = 40
GZ = 48
NC = 64
NYS = 65
NZS = 69
NXS = 77
NSEM = 82


def dot(a, b):
    return lax.dot_general(a, b, (((1,), (0,)), ((), ())), preferred_element_type=F32)


def dot_nt(a, b):
    return lax.dot_general(a, b, (((1,), (1,)), ((), ())), preferred_element_type=F32)


def kernel(
    tokens, gain1, qkv1, out1, gain2, qkv2, out2, hpos, scene, cot,
    o_gin, o_qkv1, o_out1, o_qkv2, o_out2, o_gain,
    s_ref, st_ref, r_ref, rt_ref, bias_ref,
    h_ref, ht_ref, rinv_ref, kv_ref, kt_ref, vt_ref, q_ref, qt_ref, p_ref, pb_ref, obt_ref, ob_ref,
    do_ref, dot_ref, ds_ref, qstk_ref, dostk_ref, dqt_ref, dqkv_ref, kvs_ref, kvr_ref, ct_ref,
    rss_ref, rsr_ref, ms_ref, mr_ref, as_ref, ar_ref, ag_ref,
    g_ref, gc_ref, g2_ref, gy_ref, g3_ref, gz_ref,
    n0_ref, nc_ref, n1_ref, ny_ref, n2_ref, nz_ref, nx_ref,
    ssem, rsem,
):
    t = lax.axis_index("tok")
    x = lax.axis_index("head")
    core = lax.rem(t, 2)
    z = lax.rem(t // 2, NZ)
    y = t // (2 * NZ)
    mate = t + 1 - 2 * core
    gains, qkvs, outs = (gain1, gain2), (qkv1, qkv2), (out1, out2)

    def xdev(j):
        return {"head": lax.rem(x + j, NX)}

    def ydev(j):
        return {"tok": (lax.rem(y + j, NY) * NZ + z) * 2 + core}

    def zdev(j):
        return {"tok": (y * NZ + lax.rem(z + j, NZ)) * 2 + core}

    def remote(src, dst, sem, dev):
        return pltpu.make_async_remote_copy(
            src_ref=src, dst_ref=dst, send_sem=ssem.at[sem], recv_sem=rsem.at[sem],
            device_id=dev, device_id_type=MESH,
        )

    barrier = pltpu.get_barrier_semaphore()

    def greet(j, carry):
        pl.semaphore_signal(
            barrier, inc=1, device_id={"tok": lax.rem(t + j, NT)}, device_id_type=MESH
        )
        return carry

    lax.fori_loop(1, NT, greet, 0)
    for j in range(1, NX):
        pl.semaphore_signal(barrier, inc=1, device_id=xdev(j), device_id_type=MESH)

    sends = []

    def start(copy):
        copy.start()
        sends.append(copy)
        return copy

    def u_block(layer, b):
        if layer == 0:
            return tokens[:, b * BLK : (b + 1) * BLK].astype(F32)
        return ag_ref[0, b].astype(F32)

    def u_chunk(layer, at):
        if layer == 0:
            return tokens[:, pl.ds(pl.multiple_of(at * BLK, BLK), BLK)].astype(F32)
        return ag_ref[0, at].astype(F32)

    def cot_block(layer, b):
        return cot[:, b * BLK : (b + 1) * BLK] if layer == 1 else ag_ref[1, b]

    def cot_chunk(layer, at):
        if layer == 1:
            return cot[:, pl.ds(pl.multiple_of(at * BLK, BLK), BLK)]
        return ag_ref[1, at]

    def indices():
        lane_lt = lax.broadcasted_iota(jnp.int32, (ROWS, ROWS), 0) < lax.broadcasted_iota(
            jnp.int32, (ROWS, ROWS), 1
        )
        tri = jnp.where(lane_lt, 1.0, 0.0).astype(BF16)
        slot = lax.broadcasted_iota(jnp.int32, (NT * SLOTS, ROWS), 0).astype(F32)
        dev = lax.broadcasted_iota(jnp.int32, (NT, ROWS), 0)
        lane = lax.broadcasted_iota(jnp.int32, (NT, ROWS), 1).astype(F32)
        own = hpos[pl.ds(t, 1), :] // ROWS
        hit = jnp.where(dev == own, 1.0, 0.0)
        before = dot(hit.astype(BF16), tri)
        send_id = jnp.sum(hit * (before + dev.astype(F32) * SLOTS), axis=0, keepdims=True)
        s = jnp.where(slot == send_id, 1.0, 0.0)
        s_ref[...] = s.astype(BF16)
        st_ref[...] = s.T.astype(BF16)
        every = hpos[...]
        place = lax.rem(every, ROWS).astype(F32)
        mine = jnp.where(every // ROWS == t, 1.0, 0.0)
        rank = dot(mine.astype(BF16), tri)
        recv_id = jnp.zeros((1, ROWS), F32)
        for k in range(SLOTS):
            chosen = mine * jnp.where(rank == k, 1.0, 0.0)
            row = jnp.sum(chosen * (place + 1.0), axis=1, keepdims=True) - 1.0
            found = jnp.where(row == lane, dev.astype(F32) * SLOTS + k, 0.0)
            recv_id = recv_id + jnp.sum(found, axis=0, keepdims=True)
        r = jnp.where(slot == recv_id, 1.0, 0.0)
        rt_ref[...] = r.astype(BF16)
        r_ref[...] = r.T.astype(BF16)
        ids = scene[pl.ds(t, 1), :].astype(F32)
        for half, source in ((0, t), (1, mate)):
            row = scene[pl.ds(source, 1), :].astype(F32)
            col = jnp.broadcast_to(row, (128, ROWS)).T[:, :1]
            bias_ref[half] = jnp.where(col == ids, 0.0, -1e30)

    def normalize(layer):
        total = jnp.zeros((ROWS, 1), F32)
        for b in range(NX):
            ub = u_block(layer, b)
            total = total + jnp.sum(ub * ub, axis=1, keepdims=True)
        rinv = lax.rsqrt(total * (1.0 / (NX * BLK)) + EPS)
        rinv_ref[layer] = rinv
        for b in range(NX):
            hb = u_block(layer, b) * rinv * gains[layer][b : b + 1, :]
            h_ref[layer, :, b * BLK : (b + 1) * BLK] = hb.astype(BF16)

    def keys_values(layer):
        h = h_ref[layer]
        kv_ref[layer, 0, 0] = dot(h, qkvs[layer][1]).astype(BF16)
        kv_ref[layer, 0, 1] = dot(h, qkvs[layer][2]).astype(BF16)

    def send_kv(layer):
        return start(
            remote(kv_ref.at[layer, 0], kv_ref.at[layer, 1], KV + layer, {"tok": mate})
        )

    row_head = lax.broadcasted_iota(jnp.int32, (BLK, ROWS), 0) // HD
    lane_head = lax.broadcasted_iota(jnp.int32, (ROWS, BLK), 1) // HD

    def queries(layer):
        q = dot(h_ref[layer], qkvs[layer][0]).astype(BF16).astype(F32) * 0.125
        q_ref[layer] = q.astype(BF16)
        qt = q.T
        for n in range(HEADS):
            qt_ref[:, n * ROWS : (n + 1) * ROWS] = jnp.where(row_head == n, qt, 0.0).astype(BF16)

    def attend(layer):
        for half in range(2):
            kt_ref[layer, half] = kv_ref[layer, half, 0].T
            vt_ref[layer, half] = kv_ref[layer, half, 1].T
        for n in range(HEADS):
            cols = slice(n * ROWS, (n + 1) * ROWS)
            rows = slice(n * HD, (n + 1) * HD)
            e = []
            for half in range(2):
                scores = dot(kv_ref[layer, half, 0], qt_ref[:, cols])
                if layer == 1:
                    scores = scores + bias_ref[half]
                e.append(jnp.exp(scores))
            total = jnp.sum(e[0], axis=0, keepdims=True) + jnp.sum(e[1], axis=0, keepdims=True)
            inv = 1.0 / total
            mixed = jnp.zeros((HD, ROWS), F32)
            for half in range(2):
                p = e[half] * inv
                p_ref[layer, half, :, cols] = p
                pb = p.astype(BF16)
                pb_ref[layer, half, :, cols] = pb
                mixed = mixed + dot(vt_ref[layer, half, rows, :], pb)
            obt_ref[rows, :] = mixed.astype(BF16)
        ob_ref[layer] = obt_ref[...].T

    def turn_h(layer):
        for b in range(NX):
            ht_ref[layer, b * BLK : (b + 1) * BLK, :] = h_ref[layer, :, b * BLK : (b + 1) * BLK].T

    def pull_back_out(layer):
        acc = jnp.zeros((ROWS, BLK), F32)
        for b in range(NX):
            acc = acc + dot_nt(cot_block(layer, b), outs[layer][:, b * BLK : (b + 1) * BLK])
        do = acc.astype(BF16)
        do_ref[...] = do
        dot_ref[...] = do.T
        for n in range(HEADS):
            dostk_ref[n * ROWS : (n + 1) * ROWS, :] = jnp.where(
                lane_head == n, do.astype(F32), 0.0
            ).astype(BF16)

    def attend_back(layer):
        q = q_ref[layer].astype(F32)
        dt = dot_ref[...].astype(F32)
        for n in range(HEADS):
            cols = slice(n * ROWS, (n + 1) * ROWS)
            rows = slice(n * HD, (n + 1) * HD)
            qstk_ref[n * ROWS : (n + 1) * ROWS, :] = jnp.where(lane_head == n, q, 0.0).astype(BF16)
            only = jnp.where(row_head == n, dt, 0.0).astype(BF16)
            dp = [dot(kv_ref[layer, half, 1], only) for half in range(2)]
            p = [p_ref[layer, half, :, cols] for half in range(2)]
            r = jnp.sum(dp[0] * p[0], axis=0, keepdims=True) + jnp.sum(
                dp[1] * p[1], axis=0, keepdims=True
            )
            dq = jnp.zeros((HD, ROWS), F32)
            for half in range(2):
                ds = (p[half] * (dp[half] - r)).astype(BF16)
                ds_ref[half, :, cols] = ds
                dq = dq + dot(kt_ref[layer, half, rows, :], ds)
            dqt_ref[rows, :] = (dq * 0.125).astype(BF16)
        kvs_ref[layer, 0] = dot(ds_ref[1], qstk_ref[...]).astype(BF16)
        kvs_ref[layer, 1] = dot(pb_ref[layer, 1], dostk_ref[...]).astype(BF16)
        copy = start(
            remote(kvs_ref.at[layer], kvr_ref.at[layer], BACK + layer, {"tok": mate})
        )
        dqkv_ref[0] = dqt_ref[...].T
        dk = dot(ds_ref[0], qstk_ref[...])
        dv = dot(pb_ref[layer, 0], dostk_ref[...])
        copy.wait_recv()
        dqkv_ref[1] = (dk + kvr_ref[layer, 0].astype(F32)).astype(BF16)
        dqkv_ref[2] = (dv + kvr_ref[layer, 1].astype(F32)).astype(BF16)

    def dh_part(layer, at):
        rows = pl.ds(pl.multiple_of(at * BLK, BLK), BLK)
        acc = dot_nt(dqkv_ref[0], qkvs[layer][0, rows, :])
        acc = acc + dot_nt(dqkv_ref[1], qkvs[layer][1, rows, :])
        return acc + dot_nt(dqkv_ref[2], qkvs[layer][2, rows, :])

    def send_dh(layer):
        phase = 2 - layer
        sums = jnp.zeros((ROWS, 1), F32)
        copies = []
        own = None
        for j in (2, 1, 3, 0):
            at = lax.rem(x + j, NX)
            part = dh_part(layer, at)
            weight = u_chunk(layer, at) * gains[layer][pl.ds(at, 1), :]
            sums = sums + jnp.sum(part * weight, axis=1, keepdims=True)
            if j:
                rss_ref[phase, j] = part.astype(BF16)
                copies.append(
                    start(
                        remote(
                            rss_ref.at[phase, j], rsr_ref.at[phase, j], RS + 4 * phase + j, xdev(j)
                        )
                    )
                )
            else:
                own = part
        ms_ref[layer] = jnp.broadcast_to(sums, (ROWS, 128)).T[:8, :]
        for j in (2, 1, 3):
            copies.append(
                start(
                    remote(
                        ms_ref.at[layer], mr_ref.at[layer, j], ROWSUM + 4 * layer + j, xdev(j)
                    )
                )
            )
        rss_ref_own[layer] = own
        return copies

    rss_ref_own = {}

    def finish_dh(layer, copies):
        phase = 2 - layer
        for copy in copies:
            copy.wait_recv()
        dh = rss_ref_own[layer]
        sums = ms_ref[layer]
        for j in range(1, NX):
            dh = dh + rsr_ref[phase, j].astype(F32)
            sums = sums + mr_ref[layer, j]
        mean = jnp.broadcast_to(sums[:1, :], (128, ROWS)).T[:, :1] * (1.0 / (NX * BLK))
        u = u_chunk(layer, x)
        rinv = rinv_ref[layer]
        n0_ref[layer : layer + 1, :] = jnp.sum(dh * u * rinv, axis=0, keepdims=True)
        scaled = dh * gains[layer][pl.ds(x, 1), :]
        du = cot_chunk(layer, x).astype(F32) + rinv * (scaled - u * rinv * rinv * mean)
        return du.astype(BF16)

    def relay_out(way, table, chunk):
        a = dot(table[...], chunk)
        lo = a[:, :128].reshape(NT, SLOTS, 128)
        hi = a[:, 128:].reshape(NT, SLOTS, 128)
        as_ref[way] = jnp.concatenate([lo, hi], axis=1).astype(BF16)
        ar_ref[way, t] = as_ref[way, t]

        def push(j, carry):
            to = lax.rem(t + j, NT)
            remote(as_ref.at[way, to], ar_ref.at[way, t], A2A + way, {"tok": to}).start()
            return carry

        lax.fori_loop(1, NT, push, 0)
        every = pl.ds(0, NT - 1)
        copy = remote(as_ref.at[way, every], ar_ref.at[way, every], A2A + way, {"tok": mate})
        sends.append(copy)
        return copy

    def relay_in(way, table, copy):
        copy.wait_recv()
        a = ar_ref[way].astype(F32)
        lo = a[:, :SLOTS, :].reshape(NT * SLOTS, 128)
        hi = a[:, SLOTS:, :].reshape(NT * SLOTS, 128)
        return dot(table[...], jnp.concatenate([lo, hi], axis=1).astype(BF16)).astype(BF16)

    def spread(phase, chunk):
        ag_ref[phase, x] = chunk
        copies = []
        for j in (2, 1, 3):
            copies.append(
                start(
                    remote(ag_ref.at[phase, x], ag_ref.at[phase, x], AG + 4 * phase + j, xdev(j))
                )
            )
        return copies

    def turn_cot(layer):
        for b in range(NX):
            ct_ref[b * BLK : (b + 1) * BLK, :] = cot_block(layer, b).T

    def put_grad(layer, kind, b, value):
        parts = value.reshape(NZ, 2, 16, BLK)
        for c in range(2):
            g_ref[layer, c, b * NZ : (b + 1) * NZ, kind * 16 : (kind + 1) * 16, :] = parts[
                :, c
            ].astype(BF16)

    def out_grads(layer):
        for b in range(NX):
            put_grad(layer, 3, b, dot(ct_ref[b * BLK : (b + 1) * BLK, :], ob_ref[layer]))

    def qkv_grads(layer):
        for b in range(NX):
            left = ht_ref[layer, b * BLK : (b + 1) * BLK, :]
            for kind in range(3):
                put_grad(layer, kind, b, dot(left, dqkv_ref[kind]))

    def grads_core(layer):
        return start(
            remote(g_ref.at[layer, 1 - core], gc_ref.at[layer], GC + layer, {"tok": mate})
        )

    def grads_y(layer, copy):
        copy.wait_recv()
        copies = []
        for j in (2, 1, 3, 0):
            rows = pl.ds(lax.rem(y + j, NY) * NZ, NZ)
            value = g_ref[layer, core, rows].astype(F32) + gc_ref[layer, rows].astype(F32)
            g2_ref[layer, j] = value.astype(BF16)
            if j:
                copies.append(
                    start(
                        remote(g2_ref.at[layer, j], gy_ref.at[layer, j], GY + 4 * layer + j, ydev(j))
                    )
                )
        return copies

    def grads_z(layer, copies):
        for copy in copies:
            copy.wait_recv()
        later = []
        for j in (4, 3, 5, 2, 6, 1, 7, 0):
            at = lax.rem(z + j, NZ)
            value = g2_ref[layer, 0, at].astype(F32)
            for k in range(1, NY):
                value = value + gy_ref[layer, k, at].astype(F32)
            g3_ref[layer, j] = value.astype(BF16)
            if j:
                later.append(
                    start(
                        remote(g3_ref.at[layer, j], gz_ref.at[layer, j], GZ + 8 * layer + j, zdev(j))
                    )
                )
        return later

    def grads_end(layer, copies):
        for copy in copies:
            copy.wait_recv()
        value = g3_ref[layer, 0].astype(F32)
        for j in range(1, NZ):
            value = value + gz_ref[layer, j].astype(F32)
        value = value * GRAD_SCALE
        o_qkv, o_out = ((o_qkv1, o_out1), (o_qkv2, o_out2))[layer]
        for kind in range(3):
            o_qkv[kind] = value[kind * 16 : (kind + 1) * 16, :]
        o_out[...] = value[48:64, :]

    normalize(0)
    keys_values(0)
    pl.semaphore_wait(barrier, NT - 1 + NX - 1)
    kv_copy = send_kv(0)
    queries(0)
    turn_h(0)
    indices()
    n0_ref[...] = jnp.zeros_like(n0_ref)
    kv_copy.wait_recv()
    attend(0)
    copies = []
    own = None
    for j in (2, 1, 3, 0):
        at = pl.multiple_of(lax.rem(x + j, NX) * BLK, BLK)
        part = dot(ob_ref[0], out1[:, pl.ds(at, BLK)])
        if j:
            rss_ref[0, j] = part.astype(BF16)
            copies.append(start(remote(rss_ref.at[0, j], rsr_ref.at[0, j], RS + j, xdev(j))))
        else:
            own = part
    y1 = own
    for copy in copies:
        copy.wait_recv()
    for j in range(1, NX):
        y1 = y1 + rsr_ref[0, j].astype(F32)
    y1 = (u_chunk(0, x) + y1).astype(BF16)
    relay = relay_out(0, s_ref, y1)
    pull_back_out(1)
    turn_cot(1)
    copies = spread(0, relay_in(0, r_ref, relay))
    for copy in copies:
        copy.wait_recv()

    normalize(1)
    keys_values(1)
    kv_copy = send_kv(1)
    queries(1)
    turn_h(1)
    kv_copy.wait_recv()
    attend(1)
    attend_back(1)
    copies = send_dh(1)
    out_grads(1)
    qkv_grads(1)
    core_copy = grads_core(1)
    du2 = finish_dh(1, copies)
    relay = relay_out(1, rt_ref, du2)
    y_copies = grads_y(1, core_copy)
    copies = spread(1, relay_in(1, st_ref, relay))
    z_copies = grads_z(1, y_copies)
    for copy in copies:
        copy.wait_recv()

    pull_back_out(0)
    attend_back(0)
    copies = send_dh(0)
    grads_end(1, z_copies)
    turn_cot(0)
    out_grads(0)
    qkv_grads(0)
    core_copy = grads_core(0)
    du1 = finish_dh(0, copies)
    copies = spread(2, du1)
    gain_copy = start(remote(n0_ref, nc_ref, NC, {"tok": mate}))
    y_copies = grads_y(0, core_copy)
    gain_copy.wait_recv()
    n1_ref[...] = n0_ref[...] + nc_ref[...]
    gain_copies = [start(remote(n1_ref, ny_ref.at[j], NYS + j, ydev(j))) for j in range(1, NY)]
    for copy in copies:
        copy.wait_recv()
    for b in range(NX):
        o_gin[:, b * BLK : (b + 1) * BLK] = ag_ref[2, b]
    for copy in gain_copies:
        copy.wait_recv()
    n2_ref[...] = n1_ref[...] + ny_ref[1] + ny_ref[2] + ny_ref[3]
    gain_copies = [start(remote(n2_ref, nz_ref.at[j], NZS + j, zdev(j))) for j in range(1, NZ)]
    z_copies = grads_z(0, y_copies)
    for copy in gain_copies:
        copy.wait_recv()
    value = n2_ref[...]
    for j in range(1, NZ):
        value = value + nz_ref[j]
    nx_ref[x] = value * GRAD_SCALE
    gain_copies = [start(remote(nx_ref.at[x], nx_ref.at[x], NXS + j, xdev(j))) for j in range(1, NX)]
    grads_end(0, z_copies)
    for copy in gain_copies:
        copy.wait_recv()
    o_gain[...] = nx_ref[t // (NT // NX)]
    for copy in sends:
        copy.wait_send()


def scratch():
    def b16(*shape):
        return pltpu.VMEM(shape, BF16)

    def f32(*shape):
        return pltpu.VMEM(shape, F32)

    wide = NT * SLOTS
    return [
        b16(wide, ROWS), b16(ROWS, wide), b16(ROWS, wide), b16(wide, ROWS), f32(2, ROWS, ROWS),
        b16(2, ROWS, NX * BLK), b16(2, NX * BLK, ROWS), f32(2, ROWS, 1),
        b16(2, 2, 2, ROWS, BLK), b16(2, 2, BLK, ROWS), b16(2, 2, BLK, ROWS),
        b16(2, ROWS, BLK), b16(BLK, HEADS * ROWS), f32(2, 2, ROWS, HEADS * ROWS),
        b16(2, 2, ROWS, HEADS * ROWS), b16(BLK, ROWS), b16(2, ROWS, BLK),
        b16(ROWS, BLK), b16(BLK, ROWS), b16(2, ROWS, HEADS * ROWS), b16(HEADS * ROWS, BLK),
        b16(HEADS * ROWS, BLK), b16(BLK, ROWS), b16(3, ROWS, BLK), b16(2, 2, ROWS, BLK),
        b16(2, 2, ROWS, BLK), b16(NX * BLK, ROWS),
        b16(3, NX, ROWS, BLK), b16(3, NX, ROWS, BLK), f32(2, 8, ROWS), f32(2, NX, 8, ROWS),
        b16(2, NT, 2 * SLOTS, 128), b16(2, NT, 2 * SLOTS, 128), b16(3, NX, ROWS, BLK),
        b16(2, 2, NY * NZ, 64, BLK), b16(2, NY * NZ, 64, BLK), b16(2, NY, NZ, 64, BLK),
        b16(2, NY, NZ, 64, BLK), b16(2, NZ, 64, BLK), b16(2, NZ, 64, BLK),
        f32(8, BLK), f32(8, BLK), f32(8, BLK), f32(NY, 8, BLK), f32(8, BLK), f32(NZ, 8, BLK),
        f32(NX, 8, BLK),
        pltpu.SemaphoreType.DMA((NSEM,)), pltpu.SemaphoreType.DMA((NSEM,)),
    ]


def local(
    tokens, gain_one, qkv_one, out_one, gain_two, qkv_two, out_two, hilbert_pos, scene, cotangent
):
    vmem = pl.BlockSpec(memory_space=pltpu.VMEM)
    grads = [
        jax.ShapeDtypeStruct((3, 16, BLK), F32),
        jax.ShapeDtypeStruct((16, BLK), F32),
    ]
    grad_input, qkv1, out1, qkv2, out2, gains = pl.pallas_call(
        kernel,
        out_shape=[
            jax.ShapeDtypeStruct((ROWS, NX * BLK), BF16),
            *grads,
            *grads,
            jax.ShapeDtypeStruct((8, BLK), F32),
        ],
        in_specs=[vmem] * 10,
        out_specs=[vmem] * 6,
        scratch_shapes=scratch(),
        compiler_params=pltpu.CompilerParams(
            collective_id=0, has_side_effects=True, vmem_limit_bytes=58 * 2**20
        ),
    )(
        tokens,
        gain_one.reshape(NX, BLK),
        qkv_one,
        out_one,
        gain_two.reshape(NX, BLK),
        qkv_two,
        out_two,
        hilbert_pos.reshape(NT, ROWS),
        scene.reshape(NT, ROWS),
        cotangent,
    )
    at = lax.rem(lax.axis_index("tok"), NT // NX) * 16
    mine = lax.dynamic_slice(gains, (0, at), (2, 16))
    return grad_input, qkv1, out1, mine[0], qkv2, out2, mine[1]


def solution(mesh):
    in_specs = (
        P("tok", None),
        P(),
        P(None, None, "head"),
        P("head", None),
        P(),
        P(None, None, "head"),
        P("head", None),
        P(),
        P(),
        P("tok", None),
    )
    out_specs = (
        P("tok", None),
        P(None, "tok", "head"),
        P("tok", "head"),
        P("tok"),
        P(None, "tok", "head"),
        P("tok", "head"),
        P("tok"),
    )
    return jax.shard_map(local, mesh=mesh, in_specs=in_specs, out_specs=out_specs, check_vma=False)
```

time: 981 us -> 134 us (0.14); the launches traced: 968 us -> 134 us
  waiting for transfers between devices: 573 us -> 0 us
  blocking collectives: 146 us -> 0 us
  local copies, waits for them, and re-layouts: 138 us -> 14.1 us
  Pallas kernels: 0 us -> 119 us
  matrix products: 64 us -> 0 us
  starting transfers between devices: 17.2 us -> 0 us
  between operations: 16.1 us -> 0.66 us
  other arithmetic: 14.6 us -> 0 us
    reduce_scatter x3 -> x0, waiting for transfers between devices: 434 us -> none  [the longest x2 292 us: layer_back(): lax.psum_scatter(qkv_grad, 'tok', scatter_dimension=1, tiled=True)]
    scatter x3 -> x0, local copies, waits for them, and re-layouts: 122 us -> none  [the longest x1 60.3 us: local(): jnp.zeros_like(hilbert_pos).at[hilbert_pos]]
    pallas_call x0 -> x1, Pallas kernels: none -> 119 us  [local(): pl.pallas_call(kernel, out_shape=[jax.ShapeDtypeStruct((ROWS, NX * BLK),...]
    unnamed x1 -> x0, blocking collectives: 108 us -> none
    psum x3 -> x0, waiting for transfers between devices: 81 us -> none  [mix_heads(): return lax.psum(partial_sum, 'head')]
    dot_general x35 -> x0, matrix products: 64 us -> none  [the longest x2 17.9 us: layer_back(): jnp.einsum('hqk,khd->qhd', d_low, keys_win, preferred_element_type=jnp.fl...]
    all_to_all x1 -> x0, blocking collectives: 37.5 us -> none  [relayout(): lax.all_to_all(outgoing, 'tok', split_axis=0, concat_axis=0, tiled=True)]
    unnamed x8 -> x0, waiting for transfers between devices: 32.5 us -> none
  transfers between devices with their start and end apart: 16 -> 0, of which waited for: 8 -> 0; matrix products, arithmetic and copies ran while one was open for 9% -> 0% of each run, Pallas kernels for 0% -> 0%
where the time goes in v1:
time: 134 us
  Pallas kernels  119 us (89%)
  local copies, waits for them, and re-layouts  14.1 us (11%)
    pallas_call x1, Pallas kernels, local(): pl.pallas_call(kernel, out_shape=[jax.ShapeDtypeStruct((ROWS, NX * BLK),...  119 us
    unnamed x5, local copies, waits for them, and re-layouts  7.35 us

profile of v1, /device:TPU:8, one launch (start us, length us, event | category | flops | bytes accessed | tf_op | source)
XLA Modules:
  0.0 133.5 jit_solution(11408743536381723235)
XLA Ops:
  0.6 1.5 %reshape.28.hpos = s32[64,256]{1,0:T(8,128)} reshape(s32[16384]{0:T(1024)} %param.17) | data formatting | bytes 131072 | tf_op jit(solution)/shard_map/reshape | solution.py:569
  2.1 1.5 %reshape.29.scene = s32[64,256]{1,0:T(8,128)} reshape(s32[16384]{0:T(1024)} %param.18) | data formatting | bytes 131072 | tf_op jit(solution)/shard_map/reshape | solution.py:570
  3.6 1.3 reshape.26.gain1
  4.9 1.3 reshape.27.gain2
  6.2 118.7 %shard_map.153 = (bf16[256,1024]{1,0:T(8,128)(2,1)}, f32[3,16,256]{2,1,0:T(8,128)}, f32[16,256]{1,0:T(8,128)}, f32[3,16,256]{2,1,0:T(8,128)}, f32[16,256]{1,0:T(8,128)}, /*index=5*/f32[8,256]{1,0:T(8,128)}) custom-call(bf16[256,1024]{1,0:T(8,128)(2,1)} %tokens.1, f32[4,256]{1,0:T(4,128)} %reshape.26.gain1, bf16[3,1024,256]{2,1,0:T(8,128)(2,1)} %qkv1.1, ...), custom_call_target="tpu_custom_call" | custom-call | tf_op jit(solution)/shard_map/pallas_call | solution.py:547
  124.9 0.7 constant_dynamic-slice_fusion
  125.6 0.5 slice_bitcast_fusion
  126.2 1.9 %copy.22 = bf16[256,1024]{1,0:T(8,128)(2,1)} copy(bf16[256,1024]{1,0:T(8,128)(2,1)} %get-tuple-element.28) | data formatting | bytes 1048576
  128.0 1.4 %copy.23 = f32[3,16,256]{2,1,0:T(8,128)} copy(f32[3,16,256]{2,1,0:T(8,128)} %get-tuple-element.29) | data formatting | bytes 98304
  129.5 1.3 copy.24
  130.8 1.4 %copy.25 = f32[3,16,256]{2,1,0:T(8,128)} copy(f32[3,16,256]{2,1,0:T(8,128)} %get-tuple-element.32) | data formatting | bytes 98304
  132.2 1.3 copy.26

commit v2 on v1

v2 whole, which is shorter than its diff:
```python
import jax
import jax.numpy as jnp
from jax import lax
from jax.experimental import pallas as pl
from jax.experimental.pallas import tpu as pltpu
from jax.sharding import PartitionSpec as P

MESH = pl.DeviceIdType.MESH
F32 = jnp.float32
BF16 = jnp.bfloat16
EPS = 1e-06
ROWS = 256
BLK = 256
NX = 4
NT = 64
NY = 4
NZ = 8
HEADS = 4
HD = 64
SLOTS = 8
GRAD_SCALE = 1.0 / 128.0

HALF = 128

KV = 0
BACK = 2
A2A = 4
GC = 8
ROWSUM = 12
NC = 20
NYS = 20
NXS = 24
NZS = 28
RS = 36
AG = 60
GY = 84
GZ = 100
NSEM = 132


def dot(a, b):
    return lax.dot_general(a, b, (((1,), (0,)), ((), ())), preferred_element_type=F32)


def dot_nt(a, b):
    return lax.dot_general(a, b, (((1,), (1,)), ((), ())), preferred_element_type=F32)


def kernel(
    tokens_in, gain1, qkv1_in, out1_in, gain2, qkv2_in, out2_in, hpos, scene, cot_in,
    o_gin, o_qkv1, o_out1, o_qkv2, o_out2, o_gain,
    tokens, qkv1, out1, qkv2, out2, cot,
    s_ref, st_ref, r_ref, rt_ref, bias_ref,
    h_ref, ht_ref, rinv_ref, kv_ref, kt_ref, vt_ref, q_ref, qt_ref, p_ref, pb_ref, obt_ref, ob_ref,
    do_ref, dot_ref, ds_ref, qstk_ref, dostk_ref, dqt_ref, dqkv_ref, kvs_ref, kvr_ref, ct_ref,
    rss_ref, rsr_ref, ms_ref, mr_ref, as_ref, ar_ref, ag_ref,
    g_ref, gc_ref, g2_ref, gy_ref, g3_ref, gz_ref,
    n0_ref, nc_ref, n1_ref, ny_ref, n2_ref, nz_ref, n3_ref, nx_ref,
    ssem, rsem, lsem, y_known, all_known,
):
    t = lax.axis_index("tok")
    x = lax.axis_index("head")
    core = lax.rem(t, 2)
    z = lax.rem(t // 2, NZ)
    y = t // (2 * NZ)
    mate = t + 1 - 2 * core
    gains, qkvs, outs = (gain1, gain2), (qkv1, qkv2), (out1, out2)

    def xdev(j):
        return {"head": lax.rem(x + j, NX)}

    def ydev(j):
        return {"tok": (lax.rem(y + j, NY) * NZ + z) * 2 + core}

    def zdev(j):
        return {"tok": (y * NZ + lax.rem(z + j, NZ)) * 2 + core}

    def remote(src, dst, sem, dev):
        return pltpu.make_async_remote_copy(
            src_ref=src, dst_ref=dst, send_sem=ssem.at[sem], recv_sem=rsem.at[sem],
            device_id=dev, device_id_type=MESH,
        )

    loads = [
        pltpu.make_async_copy(source, target, lsem.at[i])
        for i, (source, target) in enumerate(
            (
                (tokens_in, tokens),
                (qkv1_in, qkv1),
                (out1_in, out1),
                (qkv2_in, qkv2),
                (out2_in, out2),
                (cot_in, cot),
            )
        )
    ]
    for load in loads:
        load.start()
    barrier = pltpu.get_barrier_semaphore()

    near = [{"tok": mate}]
    near += [xdev(j) for j in range(1, NX)]
    near += [ydev(j) for j in range(1, NY)]
    near += [zdev(j) for j in range(1, NZ)]
    for dev in near:
        pl.semaphore_signal(barrier, inc=1, device_id=dev, device_id_type=MESH)

    sends = []

    def start(copy):
        copy.start()
        sends.append(copy)
        return copy

    def gathered(phase, b):
        return jnp.concatenate([ag_ref[phase, 0, b], ag_ref[phase, 1, b]], axis=1)

    def u_block(layer, b):
        if layer == 0:
            return tokens[:, b * BLK : (b + 1) * BLK].astype(F32)
        return gathered(0, b).astype(F32)

    def half_cols(at, half):
        return pl.ds(pl.multiple_of(at * BLK + half * HALF, HALF), HALF)

    def u_part(layer, at, half):
        if layer == 0:
            return tokens[:, half_cols(at, half)].astype(F32)
        return ag_ref[0, half, at].astype(F32)

    def gain_part(layer, at, half):
        return gains[layer][pl.ds(2 * at + half, 1), :]

    def cot_block(layer, b):
        return cot[:, b * BLK : (b + 1) * BLK] if layer == 1 else gathered(1, b)

    def cot_part(layer, half):
        if layer == 1:
            return cot[:, half_cols(x, half)].astype(F32)
        return ag_ref[1, half, x].astype(F32)

    def wide_row(ref, at):
        return jnp.concatenate([ref[pl.ds(2 * at, 1), :], ref[pl.ds(2 * at + 1, 1), :]], axis=1)

    def indices():
        lane_lt = lax.broadcasted_iota(jnp.int32, (ROWS, ROWS), 0) < lax.broadcasted_iota(
            jnp.int32, (ROWS, ROWS), 1
        )
        tri = jnp.where(lane_lt, 1.0, 0.0).astype(BF16)
        slot = lax.broadcasted_iota(jnp.int32, (NT * SLOTS, ROWS), 0).astype(F32)
        dev = lax.broadcasted_iota(jnp.int32, (NT, ROWS), 0)
        lane = lax.broadcasted_iota(jnp.int32, (NT, ROWS), 1).astype(F32)
        own = wide_row(hpos, t) // ROWS
        hit = jnp.where(dev == own, 1.0, 0.0)
        before = dot(hit.astype(BF16), tri)
        send_id = jnp.sum(hit * (before + dev.astype(F32) * SLOTS), axis=0, keepdims=True)
        s = jnp.where(slot == send_id, 1.0, 0.0)
        s_ref[...] = s.astype(BF16)
        st_ref[...] = s.T.astype(BF16)
        every = jnp.concatenate([hpos[0::2, :], hpos[1::2, :]], axis=1)
        place = lax.rem(every, ROWS).astype(F32)
        mine = jnp.where(every // ROWS == t, 1.0, 0.0)
        rank = dot(mine.astype(BF16), tri)
        recv_id = jnp.zeros((1, ROWS), F32)
        for k in range(SLOTS):
            chosen = mine * jnp.where(rank == k, 1.0, 0.0)
            row = jnp.sum(chosen * (place + 1.0), axis=1, keepdims=True) - 1.0
            found = jnp.where(row == lane, dev.astype(F32) * SLOTS + k, 0.0)
            recv_id = recv_id + jnp.sum(found, axis=0, keepdims=True)
        r = jnp.where(slot == recv_id, 1.0, 0.0)
        rt_ref[...] = r.astype(BF16)
        r_ref[...] = r.T.astype(BF16)
        ids = wide_row(scene, t).astype(F32)
        for half, source in ((0, t), (1, mate)):
            row = wide_row(scene, source).astype(F32)
            col = jnp.broadcast_to(row, (128, ROWS)).T[:, :1]
            bias_ref[half] = jnp.where(col == ids, 0.0, -1e30)

    def normalize(layer):
        total = jnp.zeros((ROWS, 1), F32)
        for b in range(NX):
            ub = u_block(layer, b)
            total = total + jnp.sum(ub * ub, axis=1, keepdims=True)
        rinv = lax.rsqrt(total * (1.0 / (NX * BLK)) + EPS)
        rinv_ref[layer] = rinv
        for b in range(NX):
            hb = u_block(layer, b) * rinv * wide_row(gains[layer], b)
            h_ref[layer, :, b * BLK : (b + 1) * BLK] = hb.astype(BF16)

    def keys_values(layer):
        h = h_ref[layer]
        kv_ref[layer, 0, 0] = dot(h, qkvs[layer][1]).astype(BF16)
        kv_ref[layer, 0, 1] = dot(h, qkvs[layer][2]).astype(BF16)

    def send_kv(layer):
        return start(
            remote(kv_ref.at[layer, 0], kv_ref.at[layer, 1], KV + layer, {"tok": mate})
        )

    row_head = lax.broadcasted_iota(jnp.int32, (BLK, ROWS), 0) // HD
    lane_head = lax.broadcasted_iota(jnp.int32, (ROWS, BLK), 1) // HD

    def queries(layer):
        q = dot(h_ref[layer], qkvs[layer][0]).astype(BF16).astype(F32) * 0.125
        q_ref[layer] = q.astype(BF16)
        qt = q.T
        for n in range(HEADS):
            qt_ref[:, n * ROWS : (n + 1) * ROWS] = jnp.where(row_head == n, qt, 0.0).astype(BF16)

    def attend(layer):
        for half in range(2):
            kt_ref[layer, half] = kv_ref[layer, half, 0].T
            vt_ref[layer, half] = kv_ref[layer, half, 1].T
        for n in range(HEADS):
            cols = slice(n * ROWS, (n + 1) * ROWS)
            rows = slice(n * HD, (n + 1) * HD)
            e = []
            for half in range(2):
                scores = dot(kv_ref[layer, half, 0], qt_ref[:, cols])
                if layer == 1:
                    scores = scores + bias_ref[half]
                e.append(jnp.exp(scores))
            total = jnp.sum(e[0], axis=0, keepdims=True) + jnp.sum(e[1], axis=0, keepdims=True)
            inv = 1.0 / total
            mixed = jnp.zeros((HD, ROWS), F32)
            for half in range(2):
                p = e[half] * inv
                p_ref[layer, half, :, cols] = p
                pb = p.astype(BF16)
                pb_ref[layer, half, :, cols] = pb
                mixed = mixed + dot(vt_ref[layer, half, rows, :], pb)
            obt_ref[rows, :] = mixed.astype(BF16)
        ob_ref[layer] = obt_ref[...].T

    def turn_h(layer):
        for b in range(NX):
            ht_ref[layer, b * BLK : (b + 1) * BLK, :] = h_ref[layer, :, b * BLK : (b + 1) * BLK].T

    def pull_back_out(layer):
        acc = jnp.zeros((ROWS, BLK), F32)
        for b in range(NX):
            acc = acc + dot_nt(cot_block(layer, b), outs[layer][:, b * BLK : (b + 1) * BLK])
        do = acc.astype(BF16)
        do_ref[...] = do
        dot_ref[...] = do.T
        for n in range(HEADS):
            dostk_ref[n * ROWS : (n + 1) * ROWS, :] = jnp.where(
                lane_head == n, do.astype(F32), 0.0
            ).astype(BF16)

    def attend_back(layer, early, core_copies):
        q = q_ref[layer].astype(F32)
        dt = dot_ref[...].astype(F32)
        for n in range(HEADS):
            cols = slice(n * ROWS, (n + 1) * ROWS)
            rows = slice(n * HD, (n + 1) * HD)
            qstk_ref[n * ROWS : (n + 1) * ROWS, :] = jnp.where(lane_head == n, q, 0.0).astype(BF16)
            only = jnp.where(row_head == n, dt, 0.0).astype(BF16)
            dp = [dot(kv_ref[layer, half, 1], only) for half in range(2)]
            p = [p_ref[layer, half, :, cols] for half in range(2)]
            r = jnp.sum(dp[0] * p[0], axis=0, keepdims=True) + jnp.sum(
                dp[1] * p[1], axis=0, keepdims=True
            )
            dq = jnp.zeros((HD, ROWS), F32)
            for half in range(2):
                ds = (p[half] * (dp[half] - r)).astype(BF16)
                ds_ref[half, :, cols] = ds
                dq = dq + dot(kt_ref[layer, half, rows, :], ds)
            dqt_ref[rows, :] = (dq * 0.125).astype(BF16)
        kvs_ref[layer, 0] = dot(ds_ref[1], qstk_ref[...]).astype(BF16)
        kvs_ref[layer, 1] = dot(pb_ref[layer, 1], dostk_ref[...]).astype(BF16)
        copy = start(
            remote(kvs_ref.at[layer], kvr_ref.at[layer], BACK + layer, {"tok": mate})
        )
        dqkv_ref[0] = dqt_ref[...].T
        dk = dot(ds_ref[0], qstk_ref[...])
        dv = dot(pb_ref[layer, 0], dostk_ref[...])
        if early:
            turn_cot(layer)
            early_grads(layer)
            core_copies.append(grads_core(layer, 0))
        copy.wait_recv()
        dqkv_ref[1] = (dk + kvr_ref[layer, 0].astype(F32)).astype(BF16)
        dqkv_ref[2] = (dv + kvr_ref[layer, 1].astype(F32)).astype(BF16)

    def dh_part(layer, at, half):
        rows = half_cols(at, half)
        acc = dot_nt(dqkv_ref[0], qkvs[layer][0, rows, :])
        acc = acc + dot_nt(dqkv_ref[1], qkvs[layer][1, rows, :])
        return acc + dot_nt(dqkv_ref[2], qkvs[layer][2, rows, :])

    def send_part(phase, half, j, part):
        rss_ref[phase, half, j] = part.astype(BF16)
        sem = RS + 8 * phase + 4 * half + j
        return start(remote(rss_ref.at[phase, half, j], rsr_ref.at[phase, half, j], sem, xdev(j)))

    def send_dh(layer):
        phase = 2 - layer
        sums = jnp.zeros((ROWS, 1), F32)
        copies = ([], [])
        own = [None, None]
        rinv = rinv_ref[layer]
        for half in range(2):
            for j in (2, 1, 3, 0):
                at = lax.rem(x + j, NX)
                part = dh_part(layer, at, half)
                if j:
                    copies[half].append(send_part(phase, half, j, part))
                else:
                    own[half] = part
                weighted = part * u_part(layer, at, half)
                sums = sums + jnp.sum(
                    weighted * gain_part(layer, at, half), axis=1, keepdims=True
                )
                n0_ref[at, layer : layer + 1, half * HALF : (half + 1) * HALF] = jnp.sum(
                    weighted * rinv, axis=0, keepdims=True
                )
        ms_ref[layer] = jnp.broadcast_to(sums, (ROWS, 128)).T[:8, :]
        for j in (2, 1, 3):
            sem = ROWSUM + 4 * layer + j
            copies[0].append(start(remote(ms_ref.at[layer], mr_ref.at[layer, j], sem, xdev(j))))
        return own, copies

    def row_mean(layer):
        sums = ms_ref[layer]
        for j in range(1, NX):
            sums = sums + mr_ref[layer, j]
        return jnp.broadcast_to(sums[:1, :], (128, ROWS)).T[:, :1] * (1.0 / (NX * BLK))

    def wait_all(copies):
        for copy in copies:
            copy.wait_recv()

    def total_part(phase, half, own):
        for j in range(1, NX):
            own = own + rsr_ref[phase, half, j].astype(F32)
        return own

    def finish_dh(layer, half, dh, mean):
        u = u_part(layer, x, half)
        rinv = rinv_ref[layer]
        scaled = dh * gain_part(layer, x, half)
        du = cot_part(layer, half) + rinv * (scaled - u * rinv * rinv * mean)
        return du.astype(BF16)

    def relay_out(way, half, table, chunk):
        packed = dot(table[...], chunk).reshape(NT, SLOTS, HALF)
        as_ref[way, half] = packed.astype(BF16)
        ar_ref[way, half, t] = as_ref[way, half, t]
        sem = A2A + 2 * way + half

        def push(j, carry):
            to = lax.rem(t + j, NT)
            remote(as_ref.at[way, half, to], ar_ref.at[way, half, t], sem, {"tok": to}).start()
            return carry

        lax.fori_loop(1, NT, push, 0)
        every = pl.ds(0, NT - 1)
        copy = remote(
            as_ref.at[way, half, every], ar_ref.at[way, half, every], sem, {"tok": mate}
        )
        sends.append(copy)
        return copy

    def relay_in(way, half, table, copy):
        copy.wait_recv()
        packed = ar_ref[way, half].astype(F32).reshape(NT * SLOTS, HALF).astype(BF16)
        return dot(table[...], packed).astype(BF16)

    def spread(phase, half, chunk):
        ag_ref[phase, half, x] = chunk
        place = ag_ref.at[phase, half, x]
        sem = AG + 8 * phase + 4 * half
        return [start(remote(place, place, sem + j, xdev(j))) for j in (2, 1, 3)]

    def turn_cot(layer):
        for b in range(NX):
            ct_ref[b * BLK : (b + 1) * BLK, :] = cot_block(layer, b).T

    def put_grad(layer, part, kind, b, value):
        pieces = value.reshape(NZ, 2, 16, BLK)
        for c in range(2):
            g_ref[layer, part, c, b * NZ : (b + 1) * NZ, kind * 16 : (kind + 1) * 16, :] = pieces[
                :, c
            ].astype(BF16)

    def early_grads(layer):
        for b in range(NX):
            rows = slice(b * BLK, (b + 1) * BLK)
            put_grad(layer, 0, 0, b, dot(ht_ref[layer, rows, :], dqkv_ref[0]))
            put_grad(layer, 0, 1, b, dot(ct_ref[rows, :], ob_ref[layer]))

    def late_grads(layer):
        for b in range(NX):
            left = ht_ref[layer, b * BLK : (b + 1) * BLK, :]
            put_grad(layer, 1, 0, b, dot(left, dqkv_ref[1]))
            put_grad(layer, 1, 1, b, dot(left, dqkv_ref[2]))

    def grads_core(layer, part):
        sem = GC + 2 * layer + part
        return start(
            remote(g_ref.at[layer, part, 1 - core], gc_ref.at[layer, part], sem, {"tok": mate})
        )

    def sum_core(layer, part, copy):
        copy.wait_recv()
        for j in (2, 1, 3, 0):
            rows = pl.ds(lax.rem(y + j, NY) * NZ, NZ)
            value = g_ref[layer, part, core, rows].astype(F32)
            value = value + gc_ref[layer, part, rows].astype(F32)
            g2_ref[layer, part, j] = value.astype(BF16)

    def grads_y(layer, part):
        sem = GY + 8 * layer + 4 * part
        return [
            start(remote(g2_ref.at[layer, part, j], gy_ref.at[layer, part, j], sem + j, ydev(j)))
            for j in (2, 1, 3)
        ]

    def grads_z(layer, part, copies):
        wait_all(copies)
        sem = GZ + 16 * layer + 8 * part
        later = []
        for j in (4, 3, 5, 2, 6, 1, 7, 0):
            at = lax.rem(z + j, NZ)
            value = g2_ref[layer, part, 0, at].astype(F32)
            for k in range(1, NY):
                value = value + gy_ref[layer, part, k, at].astype(F32)
            g3_ref[layer, part, j] = value.astype(BF16)
            if j:
                place = g3_ref.at[layer, part, j]
                later.append(start(remote(place, gz_ref.at[layer, part, j], sem + j, zdev(j))))
        return later

    def grads_end(layer, part, copies):
        wait_all(copies)
        value = g3_ref[layer, part, 0].astype(F32)
        for j in range(1, NZ):
            value = value + gz_ref[layer, part, j].astype(F32)
        value = value * GRAD_SCALE
        o_qkv, o_out = ((o_qkv1, o_out1), (o_qkv2, o_out2))[layer]
        if part == 0:
            o_qkv[0] = value[:16, :]
            o_out[...] = value[16:, :]
        else:
            o_qkv[1] = value[:16, :]
            o_qkv[2] = value[16:, :]

    loads[0].wait()
    normalize(0)
    loads[1].wait()
    keys_values(0)
    queries(0)
    pl.semaphore_wait(barrier, len(near))
    kv_copy = send_kv(0)
    for j in range(1, NY):
        pl.semaphore_signal(y_known, inc=1, device_id=ydev(j), device_id_type=MESH)
    turn_h(0)
    n0_ref[...] = jnp.zeros_like(n0_ref)
    kv_copy.wait_recv()
    attend(0)
    loads[2].wait()
    copies = ([], [])
    own = [None, None]
    for half in range(2):
        for j in (2, 1, 3, 0):
            part = dot(ob_ref[0], out1[:, half_cols(lax.rem(x + j, NX), half)])
            if j:
                copies[half].append(send_part(0, half, j, part))
            else:
                own[half] = part
    pl.semaphore_wait(y_known, NY - 1)
    pl.semaphore_signal(all_known, inc=1, device_id={"tok": mate}, device_id_type=MESH)
    indices()
    pl.semaphore_wait(all_known, 1)
    relays = []
    for half in range(2):
        wait_all(copies[half])
        y1 = (u_part(0, x, half) + total_part(0, half, own[half])).astype(BF16)
        relays.append(relay_out(0, half, s_ref, y1))
    for load in loads[3:]:
        load.wait()
    pull_back_out(1)
    turn_cot(1)
    copies = []
    for half in range(2):
        copies += spread(0, half, relay_in(0, half, r_ref, relays[half]))
    wait_all(copies)

    normalize(1)
    keys_values(1)
    kv_copy = send_kv(1)
    queries(1)
    turn_h(1)
    kv_copy.wait_recv()
    attend(1)
    attend_back(1, False, None)
    own, copies = send_dh(1)
    early_grads(1)
    cores_two = [grads_core(1, 0)]
    late_grads(1)
    cores_two.append(grads_core(1, 1))
    relays = []
    for half in range(2):
        wait_all(copies[half])
        if half == 0:
            mean = row_mean(1)
        du2 = finish_dh(1, half, total_part(1, half, own[half]), mean)
        relays.append(relay_out(1, half, rt_ref, du2))
    for part in range(2):
        sum_core(1, part, cores_two[part])
    copies = []
    for half in range(2):
        copies += spread(1, half, relay_in(1, half, st_ref, relays[half]))
    ys_two = [grads_y(1, part) for part in range(2)]
    wait_all(copies)

    pull_back_out(0)
    cores_one = []
    attend_back(0, True, cores_one)
    late_grads(0)
    cores_one.append(grads_core(0, 1))
    sum_core(0, 0, cores_one[0])
    ys_one = [grads_y(0, 0)]
    own, copies = send_dh(0)
    gain_copies = [start(remote(n0_ref, nc_ref, NC, {"tok": mate}))]
    sum_core(0, 1, cores_one[1])
    ys_one.append(grads_y(0, 1))
    zs_two = [grads_z(1, part, ys_two[part]) for part in range(2)]
    wait_all(gain_copies)
    n1_ref[...] = n0_ref[...] + nc_ref[...]
    gain_copies = [
        start(remote(n1_ref.at[lax.rem(y + j, NY)], ny_ref.at[j], NYS + j, ydev(j)))
        for j in range(1, NY)
    ]
    gathers = []
    for half in range(2):
        wait_all(copies[half])
        if half == 0:
            mean = row_mean(0)
        gathers += spread(2, half, finish_dh(0, half, total_part(2, half, own[half]), mean))
    wait_all(gain_copies)
    n2_ref[...] = n1_ref[y] + ny_ref[1] + ny_ref[2] + ny_ref[3]
    gain_copies = [start(remote(n2_ref, nz_ref.at[j], NZS + j, zdev(j))) for j in range(1, NZ)]
    zs_one = [grads_z(0, 0, ys_one[0])]
    for part in range(2):
        grads_end(1, part, zs_two[part])
    zs_one.append(grads_z(0, 1, ys_one[1]))
    wait_all(gain_copies)
    value = n2_ref[...]
    for j in range(1, NZ):
        value = value + nz_ref[j]
    n3_ref[...] = value
    gain_copies = [start(remote(n3_ref, nx_ref.at[j], NXS + j, xdev(j))) for j in range(1, NX)]
    wait_all(gathers)
    for b in range(NX):
        o_gin[:, b * BLK : (b + 1) * BLK] = gathered(2, b)
    wait_all(gain_copies)
    o_gain[...] = (n3_ref[...] + nx_ref[1] + nx_ref[2] + nx_ref[3]) * GRAD_SCALE
    for part in range(2):
        grads_end(0, part, zs_one[part])
    for copy in sends:
        copy.wait_send()


def deliver(
    gin, qkv1, out1, qkv2, out2, gains, o_gin, o_qkv1, o_out1, o_gain1, o_qkv2, o_out2, o_gain2
):
    pairs = ((gin, o_gin), (qkv1, o_qkv1), (out1, o_out1), (qkv2, o_qkv2), (out2, o_out2))
    for a, b in pairs:
        b[...] = a[...]
    at = lax.rem(lax.axis_index("tok"), NT // NX) * 16
    mine = pltpu.roll(gains[...], lax.rem(BLK - at, BLK), 1)
    o_gain1[...] = mine[0, :16]
    o_gain2[...] = mine[1, :16]


def scratch():
    def b16(*shape):
        return pltpu.VMEM(shape, BF16)

    def f32(*shape):
        return pltpu.VMEM(shape, F32)

    wide = NT * SLOTS
    width = NX * BLK
    return [
        b16(ROWS, width), b16(3, width, BLK), b16(BLK, width),
        b16(3, width, BLK), b16(BLK, width), b16(ROWS, width),
        b16(wide, ROWS), b16(ROWS, wide), b16(ROWS, wide), b16(wide, ROWS), f32(2, ROWS, ROWS),
        b16(2, ROWS, NX * BLK), b16(2, NX * BLK, ROWS), f32(2, ROWS, 1),
        b16(2, 2, 2, ROWS, BLK), b16(2, 2, BLK, ROWS), b16(2, 2, BLK, ROWS),
        b16(2, ROWS, BLK), b16(BLK, HEADS * ROWS), f32(2, 2, ROWS, HEADS * ROWS),
        b16(2, 2, ROWS, HEADS * ROWS), b16(BLK, ROWS), b16(2, ROWS, BLK),
        b16(ROWS, BLK), b16(BLK, ROWS), b16(2, ROWS, HEADS * ROWS), b16(HEADS * ROWS, BLK),
        b16(HEADS * ROWS, BLK), b16(BLK, ROWS), b16(3, ROWS, BLK), b16(2, 2, ROWS, BLK),
        b16(2, 2, ROWS, BLK), b16(NX * BLK, ROWS),
        b16(3, 2, NX, ROWS, HALF), b16(3, 2, NX, ROWS, HALF), f32(2, 8, ROWS), f32(2, NX, 8, ROWS),
        b16(2, 2, NT, SLOTS, HALF), b16(2, 2, NT, SLOTS, HALF), b16(3, 2, NX, ROWS, HALF),
        b16(2, 2, 2, NY * NZ, 32, BLK), b16(2, 2, NY * NZ, 32, BLK), b16(2, 2, NY, NZ, 32, BLK),
        b16(2, 2, NY, NZ, 32, BLK), b16(2, 2, NZ, 32, BLK), b16(2, 2, NZ, 32, BLK),
        f32(NX, 8, BLK), f32(NX, 8, BLK), f32(NX, 8, BLK), f32(NY, 8, BLK), f32(8, BLK),
        f32(NZ, 8, BLK), f32(8, BLK), f32(NX, 8, BLK),
        pltpu.SemaphoreType.DMA((NSEM,)), pltpu.SemaphoreType.DMA((NSEM,)),
        pltpu.SemaphoreType.DMA((6,)), pltpu.SemaphoreType.REGULAR, pltpu.SemaphoreType.REGULAR,
    ]


def local(
    tokens, gain_one, qkv_one, out_one, gain_two, qkv_two, out_two, hilbert_pos, scene, cotangent
):
    vmem = pl.BlockSpec(memory_space=pltpu.VMEM)
    hbm = pl.BlockSpec(memory_space=pl.ANY)
    grads = [
        jax.ShapeDtypeStruct((3, 16, BLK), F32),
        jax.ShapeDtypeStruct((16, BLK), F32),
    ]
    grad_input, qkv1, out1, qkv2, out2, gains = pl.pallas_call(
        kernel,
        out_shape=[
            jax.ShapeDtypeStruct((ROWS, NX * BLK), BF16),
            *grads,
            *grads,
            jax.ShapeDtypeStruct((8, BLK), F32),
        ],
        in_specs=[hbm, vmem, hbm, hbm, vmem, hbm, hbm, vmem, vmem, hbm],
        out_specs=[vmem] * 6,
        scratch_shapes=scratch(),
        compiler_params=pltpu.CompilerParams(
            collective_id=0, has_side_effects=True, vmem_limit_bytes=58 * 2**20
        ),
    )(
        tokens,
        gain_one.reshape(2 * NX, 128),
        qkv_one,
        out_one,
        gain_two.reshape(2 * NX, 128),
        qkv_two,
        out_two,
        hilbert_pos.reshape(2 * NT, 128),
        scene.reshape(2 * NT, 128),
        cotangent,
    )
    small = jax.ShapeDtypeStruct((16,), F32)
    grad_input, qkv1, out1, gain1, qkv2, out2, gain2 = pl.pallas_call(
        deliver,
        out_shape=[
            jax.ShapeDtypeStruct((ROWS, NX * BLK), BF16),
            *grads,
            small,
            *grads,
            small,
        ],
        in_specs=[vmem] * 6,
        out_specs=[vmem] * 7,
    )(grad_input, qkv1, out1, qkv2, out2, gains)
    return grad_input, qkv1, out1, gain1, qkv2, out2, gain2


def solution(mesh):
    in_specs = (
        P("tok", None),
        P(),
        P(None, None, "head"),
        P("head", None),
        P(),
        P(None, None, "head"),
        P("head", None),
        P(),
        P(),
        P("tok", None),
    )
    out_specs = (
        P("tok", None),
        P(None, "tok", "head"),
        P("tok", "head"),
        P("tok"),
        P(None, "tok", "head"),
        P("tok", "head"),
        P("tok"),
    )
    return jax.shard_map(local, mesh=mesh, in_specs=in_specs, out_specs=out_specs, check_vma=False)
```

time: 134 us -> 104 us (0.78); the launches traced: 134 us -> 102 us
  Pallas kernels: 119 us -> 101 us
  local copies, waits for them, and re-layouts: 14.1 us -> 0 us
    pallas_call x1, Pallas kernels: 119 us -> 99.4 us  [local(): pl.pallas_call(kernel, out_shape=[jax.ShapeDtypeStruct((ROWS, NX * BLK),...]
    unnamed x5 -> x0, local copies, waits for them, and re-layouts: 7.35 us -> none
    reshape x4 -> x0, local copies, waits for them, and re-layouts: 5.53 us -> none  [the longest x1 1.49 us: local(): hilbert_pos.reshape(NT, ROWS)]
    pallas_call x0 -> x1, Pallas kernels: none -> 1.96 us  [local(): pl.pallas_call(deliver, out_shape=[jax.ShapeDtypeStruct((ROWS, NX * BLK),...]
where the time goes in v2:
time: 104 us; the launch traced here: 102 us
  Pallas kernels  101 us (97%)
    pallas_call x1, Pallas kernels, local(): pl.pallas_call(kernel, out_shape=[jax.ShapeDtypeStruct((ROWS, NX * BLK),...  99.4 us

profile of v2, /device:TPU:8, one launch (start us, length us, event | category | flops | bytes accessed | tf_op | source)
XLA Modules:
  0.0 102.0 jit_solution(9965317431519252761)
XLA Ops:
  0.6 99.4 %shard_map.153 = (bf16[256,1024]{1,0:T(8,128)(2,1)}, f32[3,16,256]{2,1,0:T(8,128)}, f32[16,256]{1,0:T(8,128)}, f32[3,16,256]{2,1,0:T(8,128)}, f32[16,256]{1,0:T(8,128)}, /*index=5*/f32[8,256]{1,0:T(8,128)}) custom-call(bf16[256,1024]{1,0:T(8,128)(2,1)} %tokens_in.1, f32[8,128]{1,0:T(8,128)} %bitcast.6, bf16[3,1024,256]{2,1,0:T(8,128)(2,1)} %qkv1_in.1, ...), custom_call_target="tpu_custom_call" | custom-call | tf_op jit(solution)/shard_map/pallas_call | solution.py:618
  100.0 2.0 %shard_map.154 = (bf16[256,1024]{1,0:T(8,128)(2,1)}, f32[3,16,256]{2,1,0:T(8,128)}, f32[16,256]{1,0:T(8,128)}, f32[16]{0:T(128)}, f32[3,16,256]{2,1,0:T(8,128)}, /*index=5*/f32[16,256]{1,0:T(8,128)}, f32[16]{0:T(128)}) custom-call(bf16[256,1024]{1,0:T(8,128)(2,1)} %get-tuple-element.13.gin, f32[3,16,256]{2,1,0:T(8,128)} %get-tuple-element.14.qkv1, ...), custom_call_target="tpu_custom_call" | custom-call | tf_op jit(solution)/shard_map/pallas_call | solution.py:645

commit v3 on v2

--- a/solution.py
+++ b/solution.py
@@ -22,10 +22,12 @@
 
 HALF = 128
 
+GROUPS = ((0, 16), (16, 16), (32, 32))
+
 KV = 0
 BACK = 2
 A2A = 4
-GC = 8
+GC = 156
 ROWSUM = 12
 NC = 20
 NYS = 20
@@ -34,8 +36,8 @@
 RS = 36
 AG = 60
 GY = 84
-GZ = 100
-NSEM = 132
+GZ = 108
+NSEM = 162
 
 
 def dot(a, b):
@@ -54,7 +56,7 @@
     h_ref, ht_ref, rinv_ref, kv_ref, kt_ref, vt_ref, q_ref, qt_ref, p_ref, pb_ref, obt_ref, ob_ref,
     do_ref, dot_ref, ds_ref, qstk_ref, dostk_ref, dqt_ref, dqkv_ref, kvs_ref, kvr_ref, ct_ref,
     rss_ref, rsr_ref, ms_ref, mr_ref, as_ref, ar_ref, ag_ref,
-    g_ref, gc_ref, g2_ref, gy_ref, g3_ref, gz_ref,
+    g_ref, gc_ref, g2_ref, gy_ref, g3_ref, gz_ref, e2_ref, ez_ref, e3_ref, ey_ref,
     n0_ref, nc_ref, n1_ref, ny_ref, n2_ref, nz_ref, n3_ref, nx_ref,
     ssem, rsem, lsem, y_known, all_known,
 ):
@@ -94,8 +96,8 @@
             )
         )
     ]
-    for load in loads:
-        load.start()
+    loads[0].start()
+    loads[1].start()
     barrier = pltpu.get_barrier_semaphore()
 
     near = [{"tok": mate}]
@@ -248,7 +250,7 @@
                 lane_head == n, do.astype(F32), 0.0
             ).astype(BF16)
 
-    def attend_back(layer, early, core_copies):
+    def attend_back(layer, meanwhile):
         q = q_ref[layer].astype(F32)
         dt = dot_ref[...].astype(F32)
         for n in range(HEADS):
@@ -275,10 +277,7 @@
         dqkv_ref[0] = dqt_ref[...].T
         dk = dot(ds_ref[0], qstk_ref[...])
         dv = dot(pb_ref[layer, 0], dostk_ref[...])
-        if early:
-            turn_cot(layer)
-            early_grads(layer)
-            core_copies.append(grads_core(layer, 0))
+        meanwhile()
         copy.wait_recv()
         dqkv_ref[1] = (dk + kvr_ref[layer, 0].astype(F32)).astype(BF16)
         dqkv_ref[2] = (dv + kvr_ref[layer, 1].astype(F32)).astype(BF16)
@@ -373,82 +372,150 @@
         sem = AG + 8 * phase + 4 * half
         return [start(remote(place, place, sem + j, xdev(j))) for j in (2, 1, 3)]
 
-    def turn_cot(layer):
+    def turn_cot():
+        for half in range(2):
+            for b in range(NX):
+                at = b * BLK + half * HALF
+                ct_ref[half, b * HALF : (b + 1) * HALF, :] = cot[:, at : at + HALF].T
+
+    def put_grad(layer, kind, chip, value):
+        n = value.shape[0] // 32
+        pieces = value.reshape(n, 2, 16, BLK)
+        for c in range(2):
+            g_ref[layer, c, chip : chip + n, kind * 16 : (kind + 1) * 16, :] = pieces[:, c].astype(
+                BF16
+            )
+
+    def out_grads(layer, half):
         for b in range(NX):
-            ct_ref[b * BLK : (b + 1) * BLK, :] = cot_block(layer, b).T
-
-    def put_grad(layer, part, kind, b, value):
-        pieces = value.reshape(NZ, 2, 16, BLK)
-        for c in range(2):
-            g_ref[layer, part, c, b * NZ : (b + 1) * NZ, kind * 16 : (kind + 1) * 16, :] = pieces[
-                :, c
-            ].astype(BF16)
-
-    def early_grads(layer):
-        for b in range(NX):
-            rows = slice(b * BLK, (b + 1) * BLK)
-            put_grad(layer, 0, 0, b, dot(ht_ref[layer, rows, :], dqkv_ref[0]))
-            put_grad(layer, 0, 1, b, dot(ct_ref[rows, :], ob_ref[layer]))
-
-    def late_grads(layer):
+            if layer == 0:
+                left = ag_ref[1, half, b].T
+            else:
+                left = ct_ref[half, b * HALF : (b + 1) * HALF, :]
+            put_grad(layer, 0, b * NZ + half * (NZ // 2), dot(left, ob_ref[layer]))
+
+    def qkv_grads(layer, kinds):
         for b in range(NX):
             left = ht_ref[layer, b * BLK : (b + 1) * BLK, :]
-            put_grad(layer, 1, 0, b, dot(left, dqkv_ref[1]))
-            put_grad(layer, 1, 1, b, dot(left, dqkv_ref[2]))
-
-    def grads_core(layer, part):
-        sem = GC + 2 * layer + part
+            for kind in kinds:
+                put_grad(layer, kind + 1, b * NZ, dot(left, dqkv_ref[kind]))
+
+    def rows_of(layer, group):
+        first, count = GROUPS[group]
+        return pl.ds(first, count)
+
+    def grads_core(layer, group):
+        rows = rows_of(layer, group)
         return start(
-            remote(g_ref.at[layer, part, 1 - core], gc_ref.at[layer, part], sem, {"tok": mate})
+            remote(
+                g_ref.at[layer, 1 - core, :, rows],
+                gc_ref.at[layer, :, rows],
+                GC + 3 * layer + group,
+                {"tok": mate},
+            )
         )
 
-    def sum_core(layer, part, copy):
+    def grads_y(layer, group, copy):
         copy.wait_recv()
+        rows = rows_of(layer, group)
+        sem = GY + 12 * layer + 4 * group
+        copies = []
         for j in (2, 1, 3, 0):
-            rows = pl.ds(lax.rem(y + j, NY) * NZ, NZ)
-            value = g_ref[layer, part, core, rows].astype(F32)
-            value = value + gc_ref[layer, part, rows].astype(F32)
-            g2_ref[layer, part, j] = value.astype(BF16)
-
-    def grads_y(layer, part):
-        sem = GY + 8 * layer + 4 * part
-        return [
-            start(remote(g2_ref.at[layer, part, j], gy_ref.at[layer, part, j], sem + j, ydev(j)))
-            for j in (2, 1, 3)
-        ]
-
-    def grads_z(layer, part, copies):
+            chips = pl.ds(lax.rem(y + j, NY) * NZ, NZ)
+            value = g_ref[layer, core, chips, rows].astype(F32)
+            value = value + gc_ref[layer, chips, rows].astype(F32)
+            g2_ref[layer, j, :, rows] = value.astype(BF16)
+            if j:
+                place = g2_ref.at[layer, j, :, rows]
+                copies.append(
+                    start(remote(place, gy_ref.at[layer, j, :, rows], sem + j, ydev(j)))
+                )
+        return copies
+
+    def grads_z(layer, group, copies):
         wait_all(copies)
-        sem = GZ + 16 * layer + 8 * part
+        rows = rows_of(layer, group)
+        sem = GZ + 24 * layer + 8 * group
         later = []
         for j in (4, 3, 5, 2, 6, 1, 7, 0):
             at = lax.rem(z + j, NZ)
-            value = g2_ref[layer, part, 0, at].astype(F32)
+            value = g2_ref[layer, 0, at, rows].astype(F32)
             for k in range(1, NY):
-                value = value + gy_ref[layer, part, k, at].astype(F32)
-            g3_ref[layer, part, j] = value.astype(BF16)
+                value = value + gy_ref[layer, k, at, rows].astype(F32)
+            g3_ref[layer, j, rows] = value.astype(BF16)
             if j:
-                place = g3_ref.at[layer, part, j]
-                later.append(start(remote(place, gz_ref.at[layer, part, j], sem + j, zdev(j))))
+                place = g3_ref.at[layer, j, rows]
+                later.append(start(remote(place, gz_ref.at[layer, j, rows], sem + j, zdev(j))))
         return later
 
-    def grads_end(layer, part, copies):
+    def grads_end(layer, group, copies):
         wait_all(copies)
-        value = g3_ref[layer, part, 0].astype(F32)
+        rows = rows_of(layer, group)
+        value = g3_ref[layer, 0, rows].astype(F32)
         for j in range(1, NZ):
-            value = value + gz_ref[layer, part, j].astype(F32)
+            value = value + gz_ref[layer, j, rows].astype(F32)
         value = value * GRAD_SCALE
-        o_qkv, o_out = ((o_qkv1, o_out1), (o_qkv2, o_out2))[layer]
-        if part == 0:
-            o_qkv[0] = value[:16, :]
-            o_out[...] = value[16:, :]
+        o_qkv = (o_qkv1, o_qkv2)[layer]
+        first, count = GROUPS[group]
+        for i in range(count // 16):
+            o_qkv[first // 16 + i - 1] = value[i * 16 : (i + 1) * 16, :]
+
+    def out_z(layer, copy):
+        copy.wait_recv()
+        copies = []
+        for j in (4, 3, 5, 2, 6, 1, 7, 0):
+            at = lax.rem(z + j, NZ)
+            for k in range(NY):
+                chip = k * NZ + at
+                value = g_ref[layer, core, chip, 0:16].astype(F32)
+                value = value + gc_ref[layer, chip, 0:16].astype(F32)
+                e2_ref[layer, j, k] = value.astype(BF16)
+            if j:
+                place = e2_ref.at[layer, j]
+                copies.append(
+                    start(remote(place, ez_ref.at[layer, j], GZ + 24 * layer + j, zdev(j)))
+                )
+        return copies
+
+    def out_y(layer, copies):
+        wait_all(copies)
+        later = []
+        for j in (2, 1, 3, 0):
+            at = lax.rem(y + j, NY)
+            value = e2_ref[layer, 0, at].astype(F32)
+            for k in range(1, NZ):
+                value = value + ez_ref[layer, k, at].astype(F32)
+            e3_ref[layer, j] = value.astype(BF16)
+            if j:
+                place = e3_ref.at[layer, j]
+                later.append(
+                    start(remote(place, ey_ref.at[layer, j], GY + 12 * layer + j, ydev(j)))
+                )
+        return later
+
+    def out_end(layer, copies):
+        wait_all(copies)
+        value = e3_ref[layer, 0].astype(F32)
+        for j in range(1, NY):
+            value = value + ey_ref[layer, j].astype(F32)
+        (o_out1, o_out2)[layer][...] = value * GRAD_SCALE
+
+    def hop_one(layer, group, copy):
+        return grads_y(layer, group, copy) if group else out_z(layer, copy)
+
+    def hop_two(layer, group, copies):
+        return grads_z(layer, group, copies) if group else out_y(layer, copies)
+
+    def hops_end(layer, group, copies):
+        if group:
+            grads_end(layer, group, copies)
         else:
-            o_qkv[1] = value[:16, :]
-            o_qkv[2] = value[16:, :]
+            out_end(layer, copies)
 
     loads[0].wait()
     normalize(0)
     loads[1].wait()
+    loads[2].start()
     keys_values(0)
     queries(0)
     pl.semaphore_wait(barrier, len(near))
@@ -458,6 +525,8 @@
     turn_h(0)
     n0_ref[...] = jnp.zeros_like(n0_ref)
     kv_copy.wait_recv()
+    for load in loads[3:]:
+        load.start()
     attend(0)
     loads[2].wait()
     copies = ([], [])
@@ -481,7 +550,7 @@
     for load in loads[3:]:
         load.wait()
     pull_back_out(1)
-    turn_cot(1)
+    turn_cot()
     copies = []
     for half in range(2):
         copies += spread(0, half, relay_in(0, half, r_ref, relays[half]))
@@ -494,12 +563,21 @@
     turn_h(1)
     kv_copy.wait_recv()
     attend(1)
-    attend_back(1, False, None)
+    cores_two = []
+
+    def meanwhile_two():
+        for half in range(2):
+            out_grads(1, half)
+        cores_two.append(grads_core(1, 0))
+
+    attend_back(1, meanwhile_two)
     own, copies = send_dh(1)
-    early_grads(1)
-    cores_two = [grads_core(1, 0)]
-    late_grads(1)
+    qkv_grads(1, (0,))
     cores_two.append(grads_core(1, 1))
+    ys_two = [hop_one(1, 0, cores_two[0])]
+    qkv_grads(1, (1, 2))
+    cores_two.append(grads_core(1, 2))
+    ys_two.append(hop_one(1, 1, cores_two[1]))
     relays = []
     for half in range(2):
         wait_all(copies[half])
@@ -507,32 +585,41 @@
             mean = row_mean(1)
         du2 = finish_dh(1, half, total_part(1, half, own[half]), mean)
         relays.append(relay_out(1, half, rt_ref, du2))
-    for part in range(2):
-        sum_core(1, part, cores_two[part])
     copies = []
     for half in range(2):
-        copies += spread(1, half, relay_in(1, half, st_ref, relays[half]))
-    ys_two = [grads_y(1, part) for part in range(2)]
-    wait_all(copies)
-
+        copies.append(spread(1, half, relay_in(1, half, st_ref, relays[half])))
+    ys_two.append(hop_one(1, 2, cores_two[2]))
+    zs_two = [hop_two(1, group, ys_two[group]) for group in range(2)]
+
+    for half in range(2):
+        wait_all(copies[half])
+        out_grads(0, half)
+    cores_one = [grads_core(0, 0)]
     pull_back_out(0)
-    cores_one = []
-    attend_back(0, True, cores_one)
-    late_grads(0)
-    cores_one.append(grads_core(0, 1))
-    sum_core(0, 0, cores_one[0])
-    ys_one = [grads_y(0, 0)]
+    ys_one = []
+
+    def meanwhile_one():
+        qkv_grads(0, (0,))
+        cores_one.append(grads_core(0, 1))
+        ys_one.append(hop_one(0, 0, cores_one[0]))
+
+    attend_back(0, meanwhile_one)
+    qkv_grads(0, (1, 2))
+    cores_one.append(grads_core(0, 2))
+    ys_one.append(hop_one(0, 1, cores_one[1]))
+    zs_two.append(hop_two(1, 2, ys_two[2]))
     own, copies = send_dh(0)
     gain_copies = [start(remote(n0_ref, nc_ref, NC, {"tok": mate}))]
-    sum_core(0, 1, cores_one[1])
-    ys_one.append(grads_y(0, 1))
-    zs_two = [grads_z(1, part, ys_two[part]) for part in range(2)]
+    ys_one.append(hop_one(0, 2, cores_one[2]))
     wait_all(gain_copies)
     n1_ref[...] = n0_ref[...] + nc_ref[...]
     gain_copies = [
         start(remote(n1_ref.at[lax.rem(y + j, NY)], ny_ref.at[j], NYS + j, ydev(j)))
         for j in range(1, NY)
     ]
+    for group in range(3):
+        hops_end(1, group, zs_two[group])
+    zs_one = [hop_two(0, group, ys_one[group]) for group in range(2)]
     gathers = []
     for half in range(2):
         wait_all(copies[half])
@@ -542,10 +629,7 @@
     wait_all(gain_copies)
     n2_ref[...] = n1_ref[y] + ny_ref[1] + ny_ref[2] + ny_ref[3]
     gain_copies = [start(remote(n2_ref, nz_ref.at[j], NZS + j, zdev(j))) for j in range(1, NZ)]
-    zs_one = [grads_z(0, 0, ys_one[0])]
-    for part in range(2):
-        grads_end(1, part, zs_two[part])
-    zs_one.append(grads_z(0, 1, ys_one[1]))
+    zs_one.append(hop_two(0, 2, ys_one[2]))
     wait_all(gain_copies)
     value = n2_ref[...]
     for j in range(1, NZ):
@@ -557,8 +641,8 @@
         o_gin[:, b * BLK : (b + 1) * BLK] = gathered(2, b)
     wait_all(gain_copies)
     o_gain[...] = (n3_ref[...] + nx_ref[1] + nx_ref[2] + nx_ref[3]) * GRAD_SCALE
-    for part in range(2):
-        grads_end(0, part, zs_one[part])
+    for group in range(3):
+        hops_end(0, group, zs_one[group])
     for copy in sends:
         copy.wait_send()
 
@@ -594,11 +678,12 @@
         b16(2, 2, ROWS, HEADS * ROWS), b16(BLK, ROWS), b16(2, ROWS, BLK),
         b16(ROWS, BLK), b16(BLK, ROWS), b16(2, ROWS, HEADS * ROWS), b16(HEADS * ROWS, BLK),
         b16(HEADS * ROWS, BLK), b16(BLK, ROWS), b16(3, ROWS, BLK), b16(2, 2, ROWS, BLK),
-        b16(2, 2, ROWS, BLK), b16(NX * BLK, ROWS),
+        b16(2, 2, ROWS, BLK), b16(2, NX * HALF, ROWS),
         b16(3, 2, NX, ROWS, HALF), b16(3, 2, NX, ROWS, HALF), f32(2, 8, ROWS), f32(2, NX, 8, ROWS),
         b16(2, 2, NT, SLOTS, HALF), b16(2, 2, NT, SLOTS, HALF), b16(3, 2, NX, ROWS, HALF),
-        b16(2, 2, 2, NY * NZ, 32, BLK), b16(2, 2, NY * NZ, 32, BLK), b16(2, 2, NY, NZ, 32, BLK),
-        b16(2, 2, NY, NZ, 32, BLK), b16(2, 2, NZ, 32, BLK), b16(2, 2, NZ, 32, BLK),
+        b16(2, 2, NY * NZ, 64, BLK), b16(2, NY * NZ, 64, BLK), b16(2, NY, NZ, 64, BLK),
+        b16(2, NY, NZ, 64, BLK), b16(2, NZ, 64, BLK), b16(2, NZ, 64, BLK),
+        b16(2, NZ, NY, 16, BLK), b16(2, NZ, NY, 16, BLK), b16(2, NY, 16, BLK), b16(2, NY, 16, BLK),
         f32(NX, 8, BLK), f32(NX, 8, BLK), f32(NX, 8, BLK), f32(NY, 8, BLK), f32(8, BLK),
         f32(NZ, 8, BLK), f32(8, BLK), f32(NX, 8, BLK),
         pltpu.SemaphoreType.DMA((NSEM,)), pltpu.SemaphoreType.DMA((NSEM,)),

time: 104 us -> 98.6 us (0.948); the launches traced: 102 us -> 98.4 us
  Pallas kernels: 101 us -> 97.8 us
    pallas_call x1, Pallas kernels: 99.4 us -> 95.8 us  [local(): pl.pallas_call(kernel, out_shape=[jax.ShapeDtypeStruct((ROWS, NX * BLK),...]
where the time goes in v3:
time: 98.6 us; the launch traced here: 98.4 us
  Pallas kernels  97.8 us (99%)
    pallas_call x1, Pallas kernels, local(): pl.pallas_call(kernel, out_shape=[jax.ShapeDtypeStruct((ROWS, NX * BLK),...  95.8 us

profile of v3, /device:TPU:8, one launch (start us, length us, event | category | flops | bytes accessed | tf_op | source)
XLA Modules:
  0.0 98.4 jit_solution(1149044679454242181)
XLA Ops:
  0.6 95.8 %shard_map.153 = (bf16[256,1024]{1,0:T(8,128)(2,1)}, f32[3,16,256]{2,1,0:T(8,128)}, f32[16,256]{1,0:T(8,128)}, f32[3,16,256]{2,1,0:T(8,128)}, f32[16,256]{1,0:T(8,128)}, /*index=5*/f32[8,256]{1,0:T(8,128)}) custom-call(bf16[256,1024]{1,0:T(8,128)(2,1)} %tokens_in.1, f32[8,128]{1,0:T(8,128)} %bitcast.6, bf16[3,1024,256]{2,1,0:T(8,128)(2,1)} %qkv1_in.1, ...), custom_call_target="tpu_custom_call" | custom-call | tf_op jit(solution)/shard_map/pallas_call | solution.py:703
  96.5 2.0 %shard_map.154 = (bf16[256,1024]{1,0:T(8,128)(2,1)}, f32[3,16,256]{2,1,0:T(8,128)}, f32[16,256]{1,0:T(8,128)}, f32[16]{0:T(128)}, f32[3,16,256]{2,1,0:T(8,128)}, /*index=5*/f32[16,256]{1,0:T(8,128)}, f32[16]{0:T(128)}) custom-call(bf16[256,1024]{1,0:T(8,128)(2,1)} %get-tuple-element.13.gin, f32[3,16,256]{2,1,0:T(8,128)} %get-tuple-element.14.qkv1, ...), custom_call_target="tpu_custom_call" | custom-call | tf_op jit(solution)/shard_map/pallas_call | solution.py:730

commit v4 on v3

--- a/solution.py
+++ b/solution.py
@@ -348,12 +348,15 @@
         ar_ref[way, half, t] = as_ref[way, half, t]
         sem = A2A + 2 * way + half
 
-        def push(j, carry):
-            to = lax.rem(t + j, NT)
-            remote(as_ref.at[way, half, to], ar_ref.at[way, half, t], sem, {"tok": to}).start()
-            return carry
-
-        lax.fori_loop(1, NT, push, 0)
+        to_y = {dy: lax.rem(y + dy, NY) for dy in (2, 1, 3, 0)}
+        to_z = {dz: lax.rem(z + dz, NZ) for dz in (4, 3, 5, 2, 6, 1, 7, 0)}
+        for dy in to_y:
+            for dz in to_z:
+                for dc in (1, 0):
+                    if dy or dz or dc:
+                        to = (to_y[dy] * NZ + to_z[dz]) * 2 + (core if dc == 0 else 1 - core)
+                        place = ar_ref.at[way, half, t]
+                        remote(as_ref.at[way, half, to], place, sem, {"tok": to}).start()
         every = pl.ds(0, NT - 1)
         copy = remote(
             as_ref.at[way, half, every], ar_ref.at[way, half, every], sem, {"tok": mate}

time: 98.6 us -> 96.7 us (0.981)
  Pallas kernels: 97.8 us -> 95.5 us
    pallas_call x1, Pallas kernels: 95.8 us -> 93.5 us  [local(): pl.pallas_call(kernel, out_shape=[jax.ShapeDtypeStruct((ROWS, NX * BLK),...]
where the time goes in v4:
time: 96.7 us; the launch traced here: 96.1 us
  Pallas kernels  95.5 us (99%)
    pallas_call x1, Pallas kernels, local(): pl.pallas_call(kernel, out_shape=[jax.ShapeDtypeStruct((ROWS, NX * BLK),...  93.5 us
    pallas_call x1, Pallas kernels, local(): pl.pallas_call(deliver, out_shape=[jax.ShapeDtypeStruct((ROWS, NX * BLK),...  1.96 us

profile of v4, /device:TPU:8, one launch (start us, length us, event | category | flops | bytes accessed | tf_op | source)
XLA Modules:
  0.0 96.1 jit_solution(14537764715793146863)
XLA Ops:
  0.6 93.5 %shard_map.153 = (bf16[256,1024]{1,0:T(8,128)(2,1)}, f32[3,16,256]{2,1,0:T(8,128)}, f32[16,256]{1,0:T(8,128)}, f32[3,16,256]{2,1,0:T(8,128)}, f32[16,256]{1,0:T(8,128)}, /*index=5*/f32[8,256]{1,0:T(8,128)}) custom-call(bf16[256,1024]{1,0:T(8,128)(2,1)} %tokens_in.1, f32[8,128]{1,0:T(8,128)} %bitcast.6, bf16[3,1024,256]{2,1,0:T(8,128)(2,1)} %qkv1_in.1, ...), custom_call_target="tpu_custom_call" | custom-call | tf_op jit(solution)/shard_map/pallas_call | solution.py:706
  94.2 2.0 %shard_map.154 = (bf16[256,1024]{1,0:T(8,128)(2,1)}, f32[3,16,256]{2,1,0:T(8,128)}, f32[16,256]{1,0:T(8,128)}, f32[16]{0:T(128)}, f32[3,16,256]{2,1,0:T(8,128)}, /*index=5*/f32[16,256]{1,0:T(8,128)}, f32[16]{0:T(128)}) custom-call(bf16[256,1024]{1,0:T(8,128)(2,1)} %get-tuple-element.13.gin, f32[3,16,256]{2,1,0:T(8,128)} %get-tuple-element.14.qkv1, ...), custom_call_target="tpu_custom_call" | custom-call | tf_op jit(solution)/shard_map/pallas_call | solution.py:733
